TPU v7x, 32 devices: a whole 2x2x4 slice. The times are simulated.
32 devices in a mesh: grp: 2 (over x), tm: 16 (over z, y, core).
Axes of the slice: x: 2, y: 2, z: 4, core: 2. Of those that a mesh axis runs over, the one named last changes fastest.
Arguments:
- right_sides: float32 [64, 4, 128], P(('grp', 'tm')), parts along dimension 0, may hold values from -6 to 6
- obs_var: float32 [64, 128], P(('grp', 'tm')), parts along dimension 0, may hold values from 0.25 to 1
- footprint: bfloat16 [512, 8, 128, 128], P(('grp', 'tm')), parts along dimension 0, may hold values from -0.5 to 0.5
- tile_block: int32 [512, 8], P(('grp', 'tm')), parts along dimension 0, may hold values from 0 to 1
- tile_place: int32 [512, 8], P(('grp', 'tm')), parts along dimension 0, may hold values from 0 to 1023
- time_cov: float32 [128, 128], replicated, as said below
- lat_cov: float32 [128, 128], replicated
- lon_cov: float32 [128, 128], replicated
Outputs:
- solution: float32 [64, 4, 128], P(('grp', 'tm')), parts along dimension 0
- flux_update: float32 [256, 128, 4, 128], P(('grp', 'tm')), parts along dimension 0
There are 2 independent parts, one for each index of `grp`. A program takes and returns all parts, laid end to end along the dimension named above; an argument that names none is the same for every part. Nothing has to cross between parts.
Inputs may be any that keep to these rules, and one draw needn't show every extreme that they name: time_cov, lat_cov and lon_cov are symmetric positive definite with positive entries.
All inputs are finite; a program needn't handle non-finite values.
Results may differ from a plain program's by a relative error of at most 0.0074.
Values may be sent and summed in bfloat16 or wider, within the bound.
No kernel may reach another device: no remote copies, remote signals or barrier semaphores. Data moves between devices by JAX's collectives and lax.ppermute only.
A program may use at most 64 MiB of HBM per device.

v0:
```python
import jax
import jax.numpy as jnp
from jax import lax
from jax.experimental import pallas as pl
from jax.experimental.pallas import tpu as pltpu
from jax.sharding import PartitionSpec as P

LAT = 128
LON = 128
BLOCK_OBS = 128
SAMPLES = 4
ITERS = 2


precise = lax.Precision.HIGHEST


def solve_spd(matrix, target):
    factor = jnp.linalg.cholesky(matrix)
    halfway = lax.linalg.triangular_solve(factor, target, left_side=True, lower=True)
    return lax.linalg.triangular_solve(
        factor, halfway, left_side=True, lower=True, transpose_a=True
    )


def combine(vectors, weights):
    return jnp.einsum("nks,kj->njs", vectors, weights, precision=precise)


def gram(left, right):
    return jnp.einsum("nks,njs->kj", left, right, precision=precise)


def to_all(array):
    devices = lax.axis_size("tm")
    copies = jnp.broadcast_to(array[None], (devices,) + array.shape)
    return lax.all_to_all(copies, "tm", split_axis=0, concat_axis=0, tiled=True)


def by_gather(
    right_sides, obs_var, footprint, tile_block, tile_place, time_cov, lat_cov, lon_cov
):
    devices = lax.axis_size("tm")
    me = lax.axis_index("tm")
    owned = right_sides.shape[0]
    blocks = devices * owned
    steps_here = time_cov.shape[0] // devices
    slots = tile_block.shape[1]
    tiles = devices * slots
    rows_here = steps_here * LAT
    owner_base = (jnp.arange(devices, dtype=jnp.int32) * owned)[:, None]
    requests = owner_base + tile_block

    packed = jnp.concatenate(
        [
            right_sides.reshape(-1, 128),
            obs_var.reshape(-1, 128),
            tile_place.astype(jnp.float32).reshape(-1, 128),
        ]
    )
    everyone = to_all(packed)
    at = owned * SAMPLES
    rhs = everyone[:, :at].reshape(blocks, SAMPLES, BLOCK_OBS)
    variance = everyone[:, at : at + owned].reshape(blocks, BLOCK_OBS)
    places = everyone[:, at + owned :].reshape(devices, tiles).astype(jnp.int32)
    times = (places // LAT + steps_here * jnp.arange(devices, dtype=jnp.int32)[:, None]).reshape(-1)
    rows = (places % LAT).reshape(-1)
    time_hot = (jnp.arange(time_cov.shape[0])[:, None] == times[None, :]).astype(jnp.float32)
    row_hot = (jnp.arange(LAT)[:, None] == rows[None, :]).astype(jnp.float32)
    my_times = lax.dynamic_slice_in_dim(time_cov, me * steps_here, steps_here, 0)
    time_part = jnp.dot(my_times, time_hot, precision=precise)
    row_part = jnp.dot(lat_cov, row_hot, precision=precise)
    dense = (time_part[:, None, :] * row_part[None, :, :]).astype(jnp.bfloat16)
    dense = dense.reshape(rows_here, devices * tiles)
    mine = jnp.take(dense, tile_place.reshape(-1), axis=0)

    def spread(vectors):
        chosen = jnp.take(vectors.astype(jnp.bfloat16), requests, axis=0)
        contrib = jnp.einsum(
            "ocks,ocsl->ockl", chosen, footprint, preferred_element_type=jnp.float32
        )
        contrib = contrib.astype(jnp.bfloat16).reshape(tiles, SAMPLES * LON)
        return lax.all_gather(contrib, "tm", axis=0, tiled=True)

    def collect(gathered):
        field = jnp.dot(mine, gathered, preferred_element_type=jnp.float32)
        field = jnp.dot(field.reshape(-1, LON), lon_cov, precision=precise)
        picked = field.astype(jnp.bfloat16).reshape(devices, slots, SAMPLES, LON)
        partial = jnp.einsum(
            "ockl,ocsl->ocks", picked, footprint, preferred_element_type=jnp.float32
        )
        block_range = jnp.arange(owned, dtype=jnp.int32)
        selector = (tile_block[:, :, None] == block_range).astype(jnp.float32)
        summed = jnp.einsum("ocb,ocks->obks", selector, partial, precision=precise)
        terms = lax.all_to_all(
            summed.reshape(devices, owned * SAMPLES, BLOCK_OBS), "tm", 0, 0, tiled=True
        )
        return to_all(terms.sum(0)).reshape(blocks, SAMPLES, BLOCK_OBS)

    solution = jnp.zeros_like(rhs)
    residual = rhs
    direction = rhs
    norm_now = gram(rhs, rhs)
    gathers, sizes = [], []
    for step in range(ITERS):
        gathered = spread(direction)
        image = collect(gathered) + variance[:, None, :] * direction
        step_size = solve_spd(gram(direction, image), norm_now)
        gathers.append(gathered)
        sizes.append(step_size)
        solution = solution + combine(direction, step_size)
        if step + 1 == ITERS:
            break
        residual = residual - combine(image, step_size)
        norm_next = gram(residual, residual)
        mix_ratio = solve_spd(norm_now, norm_next)
        direction = residual + combine(direction, mix_ratio)
        norm_now = norm_next

    def mix(gathered, size):
        whole = gathered.astype(jnp.float32).reshape(-1, SAMPLES, LON)
        return jnp.einsum("tkl,kj->tjl", whole, size, precision=precise)

    def apply_dense(gathered):
        return jnp.dot(dense, gathered, preferred_element_type=jnp.float32)

    if rows_here < devices * tiles // 4:
        flux = sum(mix(apply_dense(g), size) for g, size in zip(gathers, sizes))
    else:
        total = sum(mix(g, size) for g, size in zip(gathers, sizes))
        flux = apply_dense(total.astype(jnp.bfloat16).reshape(-1, SAMPLES * LON))
    flux = jnp.dot(flux.reshape(-1, LON), lon_cov, precision=precise)
    mine_now = lax.dynamic_slice_in_dim(solution, me * owned, owned, 0)
    return (mine_now, flux.reshape(steps_here, LAT, SAMPLES, LON))


def rolled(x, shift):
    return x if shift == 0 else pltpu.roll(x, 8 - 2 * shift, x.ndim - 2)


def row_gram(left, right):
    entry = [[None] * SAMPLES for _ in range(SAMPLES)]
    for shift in range(SAMPLES):
        product = jnp.sum(left * rolled(right, shift), axis=0)
        total = jnp.broadcast_to(jnp.sum(product, axis=1, keepdims=True), product.shape)
        for k in range(SAMPLES):
            pair = total[2 * k : 2 * k + 1] + total[2 * k + 1 : 2 * k + 2]
            entry[k][(k + shift) % SAMPLES] = pair
    return entry


def row_solve(matrix, target):
    size = range(SAMPLES)
    sym = [[0.5 * (matrix[i][j] + matrix[j][i]) for j in size] for i in size]
    low = [[None] * SAMPLES for _ in size]
    scaled = [[None] * SAMPLES for _ in size]
    inverse = []
    for j in size:
        pivot = sym[j][j]
        for p in range(j):
            pivot = pivot - low[j][p] * scaled[j][p]
        inverse.append(1.0 / pivot)
        for i in range(j + 1, SAMPLES):
            value = sym[i][j]
            for p in range(j):
                value = value - scaled[i][p] * low[j][p]
            scaled[i][j] = value
            low[i][j] = value * inverse[j]
    out = [[None] * SAMPLES for _ in size]
    for c in size:
        part = []
        for i in size:
            value = target[i][c]
            for p in range(i):
                value = value - low[i][p] * part[p]
            part.append(value)
        for i in reversed(size):
            value = part[i] * inverse[i]
            for p in range(i + 1, SAMPLES):
                value = value - low[p][i] * out[p][c]
            out[i][c] = value
    return out


def row_weights(weights):
    sample = lax.broadcasted_iota(jnp.int32, (8, 128), 0) // 2
    result = []
    for shift in range(SAMPLES):
        rows = jnp.broadcast_to(weights[shift][0], (8, 128))
        for j in range(1, SAMPLES):
            rows = jnp.where(sample == j, weights[(j + shift) % SAMPLES][j], rows)
        result.append(rows)
    return result


def row_combine(x, per_shift):
    total = 0.0
    for shift in range(SAMPLES):
        total = total + rolled(x, shift) * per_shift[shift]
    return total


PIECES = 8


def fetch(source, held, arrived):
    pieces = arrived.shape[0]
    size = source.shape[0] // pieces
    copies = []
    for p in range(pieces):
        at = pl.ds(p * size, size)
        copies.append(pltpu.make_async_copy(source.at[at], held.at[at], arrived.at[p]))
    for copy in copies:
        copy.start()
    return copies


def second_of(tile_block):
    slots, owners = tile_block.shape
    tiles = owners * slots
    tile = lax.broadcasted_iota(jnp.int32, (tiles, slots), 0)
    slot = lax.broadcasted_iota(jnp.int32, (tiles, slots), 1)
    rows = jnp.dot(
        (tile % slots == slot).astype(jnp.float32),
        tile_block[...].astype(jnp.float32),
        preferred_element_type=jnp.float32,
    )
    tile = lax.broadcasted_iota(jnp.int32, (tiles, owners), 0)
    owner = lax.broadcasted_iota(jnp.int32, (tiles, owners), 1)
    return jnp.sum(jnp.where(tile // slots == owner, rows, 0.0), axis=1, keepdims=True)


def pack_body(right_sides, obs_var, tile_place, tile_block, lon, copies, mask_lon):
    slots, owners = tile_place.shape
    tiles = owners * slots
    owner = lax.broadcasted_iota(jnp.int32, (owners, tiles), 0)
    lane = lax.broadcasted_iota(jnp.int32, (owners, tiles), 1)
    spread_out = jnp.dot(
        tile_place[...].astype(jnp.float32),
        (lane // slots == owner).astype(jnp.float32),
        precision=precise,
        preferred_element_type=jnp.float32,
    )
    slot = lax.broadcasted_iota(jnp.int32, (slots, tiles), 0)
    lane = lax.broadcasted_iota(jnp.int32, (slots, tiles), 1)
    place = jnp.sum(jnp.where(lane % slots == slot, spread_out, 0.0), axis=0, keepdims=True)
    for k in range(SAMPLES):
        for b in range(2):
            copies[0, 2 * k + b : 2 * k + b + 1] = right_sides[b, k : k + 1]
    copies[0, 8:10] = obs_var[...]
    copies[0, 10:11] = place
    copies[0, 11:16] = jnp.zeros((5, tiles), jnp.float32)
    for d in range(1, copies.shape[0]):
        copies[d] = copies[0]
    mask_lon[0] = jnp.broadcast_to(second_of(tile_block), lon.shape)
    mask_lon[1] = lon[...]


def spread_tiles(vectors, held, copies, products, split):
    owners, slots = held.shape[:2]
    piece = owners // len(copies)
    for owner in range(owners):
        if owner % piece == 0:
            copies[owner // piece].wait()
        rows = vectors[owner, 0:8]
        lhs = rows.astype(jnp.bfloat16)
        if split:
            upper = lhs.astype(jnp.float32)
            lhs = jnp.concatenate([upper, rows - upper], axis=0).astype(jnp.bfloat16)
        for c in range(slots):
            r = jnp.dot(lhs, held[owner, c], preferred_element_type=jnp.float32)
            products[owner * slots + c] = r[:8] + r[8:] if split else r


def spread_end(products, mask_lon, by_column, by_tile):
    second = mask_lon[0] > 0.5
    width = by_column.shape[1]
    chunks = LON // width
    for k in range(SAMPLES):
        chosen = jnp.where(second, products[:, 2 * k + 1, :], products[:, 2 * k, :])
        mixed = jnp.dot(
            chosen, mask_lon[1], precision=precise, preferred_element_type=jnp.float32
        )
        by_tile[:, k * LON : (k + 1) * LON] = mixed.astype(jnp.bfloat16)
        turned = mixed.T.astype(jnp.bfloat16)
        by_column[k * chunks : (k + 1) * chunks] = turned.reshape(chunks, width, LON)


def first_body(
    everyone, mask_lon, footprint, by_column, by_tile, products, held, arrived
):
    copies = fetch(footprint, held, arrived)
    spread_tiles(everyone, held, copies, products, False)
    spread_end(products, mask_lon, by_column, by_tile)


def with_variance(image, everyone, vectors):
    block = lax.broadcasted_iota(jnp.int32, vectors.shape, 1) % 2
    variance = jnp.where(block == 0, everyone[:, 8:9, :], everyone[:, 9:10, :])
    return image + variance * vectors


def entries(ref):
    grid = range(SAMPLES)
    return [[ref[SAMPLES * k + j : SAMPLES * k + j + 1] for j in grid] for k in grid]


def keep(ref, matrix):
    for k in range(SAMPLES):
        for j in range(SAMPLES):
            ref[SAMPLES * k + j : SAMPLES * k + j + 1] = matrix[k][j]


def update_body(
    everyone, image_in, mask_lon, footprint, after,
    by_column, by_tile, direction, sizes, norm, products, held, arrived,
):
    del after
    copies = fetch(footprint, held, arrived)
    first = everyone[:, 0:8, :]
    image = with_variance(image_in[...], everyone, first)
    norm_now = row_gram(first, first)
    step_size = row_solve(row_gram(first, image), norm_now)
    residual = first - row_combine(image, row_weights(step_size))
    norm_next = row_gram(residual, residual)
    ratio = row_solve(norm_now, norm_next)
    direction[...] = residual + row_combine(first, row_weights(ratio))
    keep(sizes, step_size)
    keep(norm, norm_next)
    spread_tiles(direction, held, copies, products, True)
    spread_end(products, mask_lon, by_column, by_tile)


def build_body(
    me, everyone, time_cov, lat_cov,
    prior_out, parts_out, tile_prior, hot, cols, times, parts, sent, parts_sent,
):
    devices, tiles = everyone.shape[0], everyone.shape[2]
    steps_here = parts.shape[0] - LAT
    at = lax.broadcasted_iota(jnp.int32, (LAT, tiles), 0)
    for kind, cov in ((0, time_cov), (1, lat_cov)):
        whole_cov = cov[...]
        upper = whole_cov.astype(jnp.bfloat16)
        lower = (whole_cov - upper.astype(jnp.float32)).astype(jnp.bfloat16)
        ones = []
        for d in range(devices):
            place = (everyone[d, 10:11, :] + 0.5).astype(jnp.int32)
            where = place // LAT + steps_here * d if kind == 0 else place % LAT
            one = (at == where).astype(jnp.float32)
            ones.append(one.astype(jnp.bfloat16))
            turned = one.T.astype(jnp.bfloat16)
            here = slice(d * tiles, (d + 1) * tiles)
            hot[kind, here, 0:LAT] = turned
            hot[kind, here, LAT : 2 * LAT] = turned
        picked = jnp.dot(
            jnp.concatenate([upper, lower], axis=0),
            jnp.concatenate(ones, axis=1),
            preferred_element_type=jnp.float32,
        )
        cols[kind] = picked.astype(jnp.bfloat16)
        both = picked[:LAT] + picked[LAT:]
        if kind == 0:
            times[...] = both
            mine = pl.ds(pl.multiple_of(me[0] * steps_here, steps_here), steps_here)
            parts[LAT:] = times[mine, :]
        else:
            parts[:LAT] = both

    parts_copy = pltpu.make_async_copy(parts, parts_out, parts_sent)
    parts_copy.start()
    rows = tile_prior.shape[0] // PIECES

    def sending(piece):
        block = pl.ds(pl.multiple_of(piece * rows, rows), rows)
        return pltpu.make_async_copy(
            tile_prior.at[block], prior_out.at[block], sent.at[piece]
        )

    @pl.loop(0, PIECES)
    def _(piece):
        block = pl.ds(pl.multiple_of(piece * rows, rows), rows)
        by_time = jnp.dot(hot[0, block, :], cols[0], preferred_element_type=jnp.float32)
        by_row = jnp.dot(hot[1, block, :], cols[1], preferred_element_type=jnp.float32)
        tile_prior[block, :] = (by_time * by_row).astype(jnp.bfloat16)
        sending(piece).start()

    parts_copy.wait()
    for piece in range(PIECES):
        sending(piece).wait()


def mix_body(columns, tile_prior, *rest):
    mixed, total, held, arrived = rest[-4:]
    copies = fetch(tile_prior, held, arrived)
    devices, width, tiles = columns.shape
    part = devices // len(copies)
    for p, copy in enumerate(copies):
        at = range(p * part, (p + 1) * part)
        lhs = jnp.concatenate([columns[d] for d in at], axis=1)
        copy.wait()
        product = jnp.dot(
            lhs,
            held[p * part * tiles : (p + 1) * part * tiles],
            preferred_element_type=jnp.float32,
        )
        total[...] = product if p == 0 else total[...] + product
    for d in range(devices):
        mixed[d] = total[:, d * tiles : (d + 1) * tiles].astype(jnp.bfloat16)


def sum_body(terms, total, copies):
    value = jnp.sum(terms[...], axis=0)
    total[...] = value
    for d in range(copies.shape[0]):
        copies[d] = value


def collect_body(values, mask_lon, footprint, sums, rows):
    chunks = values.shape[0] // SAMPLES
    owners, slots = footprint.shape[:2]
    is_second = mask_lon[0] > 0.5
    for k in range(SAMPLES):
        turned = values[k * chunks : (k + 1) * chunks].reshape(LON, -1)
        turned = turned.astype(jnp.float32).T
        rows[:, 2 * k, :] = jnp.where(is_second, 0.0, turned)
        rows[:, 2 * k + 1, :] = jnp.where(is_second, turned, 0.0)
    for owner in range(owners):
        total = 0.0
        for c in range(slots):
            total = total + lax.dot_general(
                rows[owner * slots + c].astype(jnp.bfloat16),
                footprint[owner, c],
                (((1,), (1,)), ((), ())),
                preferred_element_type=jnp.float32,
            )
        sums[owner] = total


def flux_product_body(
    after, parts, gathered, out, token,
    ready, parts_held, held, parts_arrived, arrived, sent,
):
    del after
    (parts_copy,) = fetch(parts, parts_held, parts_arrived)
    copies = fetch(gathered, held, arrived)
    steps = parts_held.shape[0] - LAT
    half = held.shape[0] // 2
    pair = 2
    parts_copy.wait()
    sending = []
    for step in range(0, steps, pair):
        dense = []
        for t in range(step, step + pair):
            times = parts_held[LAT + t : LAT + t + 1, :]
            dense.append((times * parts_held[:LAT]).astype(jnp.bfloat16))
        dense = jnp.concatenate(dense, axis=0)
        at = pl.ds(step * LAT, pair * LAT)
        if step == 0:
            total = 0.0
            for h in range(2):
                for copy in copies[h * PIECES // 2 : (h + 1) * PIECES // 2]:
                    copy.wait()
                total = total + jnp.dot(
                    dense[:, h * half : (h + 1) * half],
                    held[h * half : (h + 1) * half],
                    preferred_element_type=jnp.float32,
                )
            ready[at] = total
            token[...] = ready[0:8, 0:128]
        else:
            ready[at] = jnp.dot(dense, held[...], preferred_element_type=jnp.float32)
        copy = pltpu.make_async_copy(ready.at[at], out.at[at], sent.at[step // pair])
        copy.start()
        sending.append(copy)
    for copy in sending:
        copy.wait()


def flux_first_body(sizes, product, out, token, ready, held, arrived, sent):
    copies = fetch(product, held, arrived)
    size = entries(sizes)
    part = held.shape[0] // len(copies)
    sending = []
    for p, copy in enumerate(copies):
        copy.wait()
        at = pl.ds(p * part, part)
        pieces = [held[at, k * LON : (k + 1) * LON] for k in range(SAMPLES)]
        for j in range(SAMPLES):
            value = 0.0
            for k in range(SAMPLES):
                value = value + pieces[k] * size[k][j]
            ready[at, j * LON : (j + 1) * LON] = value
        copy = pltpu.make_async_copy(ready.at[at], out.at[at], sent.at[p])
        copy.start()
        sending.append(copy)
    token[...] = ready[0:8, 0:128]
    for copy in sending:
        copy.wait()


def last_body(
    me, everyone, image_in, direction, sizes, norm, flux_one, flux_two,
    answer, flux, one, two, ready, one_arrived, two_arrived, sent,
):
    two_copies = fetch(flux_two, two, two_arrived)
    one_copies = fetch(flux_one, one, one_arrived)
    second = direction[...]
    image = with_variance(image_in[...], everyone, second)
    size_two = row_solve(row_gram(second, image), entries(norm))
    own = row_combine(everyone[me[0], 0:8, :], row_weights(entries(sizes)))
    own = own + row_combine(direction[me[0]], row_weights(size_two))
    for k in range(SAMPLES):
        for b in range(2):
            answer[b, k : k + 1, :] = own[2 * k + b : 2 * k + b + 1]

    steps = ready.shape[0]
    piece = steps // len(one_copies)
    sending = []
    for t in range(steps):
        if t % piece == 0:
            two_copies[t // piece].wait()
            one_copies[t // piece].wait()
        at = slice(t * LAT, (t + 1) * LAT)
        parts = [two[at, k * LON : (k + 1) * LON] for k in range(SAMPLES)]
        for j in range(SAMPLES):
            value = one[at, j * LON : (j + 1) * LON]
            for k in range(SAMPLES):
                value = value + parts[k] * size_two[k][j]
            ready[t, :, j, :] = value
        copy = pltpu.make_async_copy(ready.at[t], flux.at[t], sent.at[t])
        copy.start()
        sending.append(copy)
    for copy in sending:
        copy.wait()


MIB = 1024 * 1024


def shape_of(shape, dtype):
    return jax.ShapeDtypeStruct(shape, dtype)


def cost(flops, moved):
    return pl.CostEstimate(flops=flops, bytes_accessed=moved, transcendentals=0)


def by_columns(
    right_sides, obs_var, footprint, tile_block, tile_place, time_cov, lat_cov, lon_cov
):
    devices = lax.axis_size("tm")
    me = lax.axis_index("tm").reshape(1).astype(jnp.int32)
    steps_here = time_cov.shape[0] // devices
    tiles = tile_block.size
    every_tile = devices * tiles
    columns = SAMPLES * LON
    width = columns // devices
    rows_here = steps_here * LAT
    f32, bf16 = jnp.float32, jnp.bfloat16

    vmem = pl.BlockSpec(memory_space=pltpu.VMEM)
    smem = pl.BlockSpec(memory_space=pltpu.SMEM)
    hbm = pl.BlockSpec(memory_space=pltpu.HBM)
    vector_shape = shape_of((devices, 8, BLOCK_OBS), f32)
    column_shape = shape_of((devices, width, tiles), bf16)
    tile_shape = shape_of((tiles, columns), bf16)
    small_shape = shape_of((SAMPLES * SAMPLES, 128), f32)
    field_shape = shape_of((rows_here, columns), f32)
    parts_shape = shape_of((LAT + steps_here, every_tile), f32)
    token_shape = shape_of((8, 128), f32)
    prior_shape = shape_of((every_tile, every_tile), bf16)
    flux_shape = shape_of((steps_here, LAT, SAMPLES, LON), f32)

    def flags(count):
        return pltpu.SemaphoreType.DMA((count,))

    products = pltpu.VMEM((tiles, 8, LON), f32)
    field = pltpu.VMEM(field_shape.shape, f32)
    gathered_held = pltpu.VMEM((every_tile, columns), bf16)
    prior_held = pltpu.VMEM(prior_shape.shape, bf16)
    spread_scratch = [products, pltpu.VMEM(footprint.shape, bf16), flags(PIECES)]
    flux_scratch = [field, pltpu.VMEM(parts_shape.shape, f32), gathered_held]
    flux_scratch += [flags(1), flags(PIECES), flags(steps_here // 2)]
    tile_cost = cost(2 * 8 * footprint.size, footprint.size * 2)
    flux_cost = cost(2 * rows_here * every_tile * columns, every_tile * columns * 2)

    def call(body, in_specs, out_specs, out_shape, scratch, estimate, name, grant=53):
        return pl.pallas_call(
            body,
            in_specs=in_specs,
            out_specs=out_specs,
            out_shape=out_shape,
            scratch_shapes=scratch,
            compiler_params=pltpu.CompilerParams(vmem_limit_bytes=grant * MIB),
            cost_estimate=estimate,
            name=name,
        )

    def exchange(array):
        return lax.all_to_all(array, "tm", split_axis=0, concat_axis=0, tiled=True)

    packed, mask_lon = call(
        pack_body,
        [vmem] * 5,
        [vmem] * 2,
        [shape_of((devices, 16, 128), f32), shape_of((2, 128, 128), f32)],
        [],
        cost(0, 12 * MIB),
        "pack",
        59,
    )(right_sides, obs_var, tile_place.T, tile_block.T, lon_cov)
    everyone = exchange(packed)
    by_column, by_tile = call(
        first_body,
        [vmem, vmem, hbm],
        [vmem] * 2,
        [column_shape, tile_shape],
        spread_scratch,
        tile_cost,
        "spread_first",
    )(everyone, mask_lon, footprint)
    gathered_one = lax.all_gather(by_tile, "tm", axis=0, tiled=True)

    tile_prior, parts = call(
        build_body,
        [smem] + [vmem] * 3,
        [hbm, hbm],
        [prior_shape, parts_shape],
        [
            prior_held,
            pltpu.VMEM((2, every_tile, 2 * LAT), bf16),
            pltpu.VMEM((2, 2 * LAT, every_tile), bf16),
            pltpu.VMEM((LAT, every_tile), f32),
            pltpu.VMEM(parts_shape.shape, f32),
            flags(PIECES),
            pltpu.SemaphoreType.DMA,
        ],
        cost(4 * every_tile * every_tile * 256, every_tile * every_tile * 2),
        "build_prior",
    )(me, everyone, time_cov, lat_cov)

    def flux_product(after, gathered):
        return call(
            flux_product_body,
            [hbm, hbm, hbm],
            [hbm, vmem],
            [field_shape, token_shape],
            flux_scratch,
            flux_cost,
            "flux_product",
        )(after, parts, gathered)

    def prior(by_column, *after):
        mixed = call(
            mix_body,
            [vmem, hbm] + [hbm] * len(after),
            vmem,
            column_shape,
            [pltpu.VMEM((width, every_tile), f32), prior_held, flags(PIECES)],
            cost(2 * width * every_tile**2, every_tile**2 * 2),
            "mix_columns",
        )(exchange(by_column), tile_prior, *after)
        return exchange(mixed)

    def collect(values):
        sums = call(
            collect_body, [vmem] * 3, vmem, vector_shape, [products], tile_cost, "collect", 48
        )(values, mask_lon, footprint)
        own, copies = call(
            sum_body,
            [vmem],
            [vmem] * 2,
            [shape_of((8, BLOCK_OBS), f32), vector_shape],
            [],
            cost(0, 4 * MIB),
            "sum_terms",
        )(exchange(sums))
        return own, exchange(copies)

    own_image, image = collect(prior(by_column))
    product_one, token = flux_product(own_image, gathered_one)
    by_column, by_tile, direction, sizes, norm = call(
        update_body,
        [vmem] * 3 + [hbm] * 2,
        [vmem] * 5,
        [column_shape, tile_shape, vector_shape, small_shape, small_shape],
        spread_scratch,
        tile_cost,
        "update_spread",
    )(everyone, image, mask_lon, footprint, token)
    gathered_two = lax.all_gather(by_tile, "tm", axis=0, tiled=True)
    flux_one, token = call(
        flux_first_body,
        [vmem, hbm],
        [hbm, vmem],
        [field_shape, token_shape],
        [field, field, flags(4), flags(4)],
        cost(1 << 24, 4 * MIB),
        "flux_first",
    )(sizes, product_one)

    own_image, image = collect(prior(by_column, token))
    flux_two, _ = flux_product(own_image, gathered_two)

    answer, flux = call(
        last_body,
        [smem] + [vmem] * 5 + [hbm] * 2,
        [vmem, hbm],
        [shape_of(right_sides.shape, f32), flux_shape],
        [field, field, pltpu.VMEM(flux_shape.shape, f32), flags(4), flags(4), flags(steps_here)],
        cost(1 << 20, 6 << 20),
        "last",
    )(me, everyone, image, direction, sizes, norm, flux_one, flux_two)
    return (answer, flux)


def local(right_sides, obs_var, footprint, tile_block, tile_place, *covariances):
    devices = lax.axis_size("tm")
    tiles = tile_block.size
    fits = devices * tiles <= 2048 and devices % 4 == 0 and tiles == 128
    fits = fits and right_sides.shape[0] == 2 and (SAMPLES * LON) % (32 * devices) == 0
    fits = fits and (covariances[0].shape[0] // devices) % 4 == 0
    plan = by_columns if fits else by_gather
    return plan(right_sides, obs_var, footprint, tile_block, tile_place, *covariances)


def solution(mesh):
    in_specs = (
        P(("grp", "tm"), None, None),
        P(("grp", "tm"), None),
        P(("grp", "tm"), None, None, None),
        P(("grp", "tm"), None),
        P(("grp", "tm"), None),
        P(),
        P(),
        P(),
    )
    out_specs = (P(("grp", "tm"), None, None), P(("grp", "tm"), None, None, None))
    return jax.shard_map(local, mesh=mesh, in_specs=in_specs, out_specs=out_specs, check_vma=False)
```

profile of v0, /device:TPU:0, one launch (start us, length us, event | category | flops | bytes accessed | tf_op | source)
XLA Modules:
  0.0 150.9 jit_solution(2537320902138801100)
XLA Ops:
  7.2 0.0 all-gather.3.cloned.1.call-start
  7.2 1.8 %pack.1 = (f32[16,16,128]{2,1,0:T(8,128)}, f32[2,128,128]{2,1,0:T(8,128)}) custom-call(f32[2,4,128]{2,1,0:T(4,128)} %right_sides.1, f32[2,128]{1,0:T(2,128)} %obs_var.1, s32[8,16]{1,0:T(8,128)} %bitcast.3, s32[8,16]{1,0:T(8,128)} %bitcast.4, f32[128,128]{1,0:T(8,128)} %lon.1), custom_call_target="tpu_custom_call" | custom-call | bytes 12582912 | tf_op jit(solution)/shard_map/pack/pallas_call | solution.py:602
  9.0 15.3 %all_to_all.45.everyone = f32[16,16,128]{2,1,0:T(8,128)S(1)} all-to-all(f32[16,16,128]{2,1,0:T(8,128)} %get-tuple-element.22), channel_id=1, replica_groups=mesh['grp'=2,'tm'=16] {'tm'}, dimensions={0} | all-to-all | bytes 262144 | tf_op jit(solution)/shard_map/all_to_all | solution.py:600
  24.3 0.0 copy-start.2
  24.3 0.9 copy-done.2
  25.2 0.0 copy-start.4
  25.2 0.0 copy-start.5
  25.2 4.4 %spread_first.1 = (bf16[16,32,128]{2,1,0:T(8,128)(2,1)}, bf16[128,512]{1,0:T(8,128)(2,1)}) custom-call(f32[16,16,128]{2,1,0:T(8,128)S(1)} %all_to_all.45.everyone, f32[2,128,128]{2,1,0:T(8,128)S(1)} %copy-done.2, bf16[16,8,128,128]{3,2,1,0:T(8,128)(2,1)} %footprint.7), custom_call_target="tpu_custom_call" | custom-call | flops 33554432 | bytes 4194304 | tf_op jit(solution)/shard_map/spread_first/pallas_call | solution.py:613
  29.6 0.0 all-gather.3.cloned.1.call-update
  29.6 3.5 %all-to-all-start.1 = ((bf16[16,32,128]{2,1,0:T(8,128)(2,1)}), bf16[16,32,128]{2,1,0:T(8,128)(2,1)S(1)}, u32[]{:S(2)}, u32[]{:S(2)}) async-start(bf16[16,32,128]{2,1,0:T(8,128)(2,1)} %get-tuple-element.24), calls=%async_computation.1 | async-start | bytes 262144 | tf_op jit(solution)/shard_map/all_to_all | solution.py:600
  33.1 0.0 copy-done.4
  33.2 0.0 copy-done.5
  33.2 8.0 %build_prior.1 = (bf16[2048,2048]{1,0:T(8,128)(2,1)}, f32[136,2048]{1,0:T(8,128)}) custom-call(s32[1]{0:T(128)} %bitcast.me, f32[16,16,128]{2,1,0:T(8,128)S(1)} %all_to_all.45.everyone, f32[128,128]{1,0:T(8,128)S(1)} %copy-done.4, f32[128,128]{1,0:T(8,128)S(1)} %copy-done.5), custom_call_target="tpu_custom_call" | custom-call | flops 4294967296 | bytes 8388608 | tf_op jit(solution)/shard_map/build_prior/pallas_call | solution.py:624
  41.2 0.0 all-to-all-done.1.columns
  41.2 0.0 copy-start
  41.2 0.0 copy-start.3
  41.3 3.9 %mix_columns.2 = bf16[16,32,128]{2,1,0:T(8,128)(2,1)S(1)} custom-call(bf16[16,32,128]{2,1,0:T(8,128)(2,1)S(1)} %all-to-all-done.1.columns, bf16[2048,2048]{1,0:T(8,128)(2,1)} %get-tuple-element.25.tile_prior), custom_call_target="tpu_custom_call" | custom-call | flops 268435456 | bytes 8388608 | tf_op jit(solution)/shard_map/mix_columns/pallas_call | solution.py:654
  45.2 15.6 %all_to_all.46.values = bf16[16,32,128]{2,1,0:T(8,128)(2,1)S(1)} all-to-all(bf16[16,32,128]{2,1,0:T(8,128)(2,1)S(1)} %mix_columns.2), channel_id=1, replica_groups=mesh['grp'=2,'tm'=16] {'tm'}, dimensions={0} | all-to-all | bytes 262144 | tf_op jit(solution)/shard_map/all_to_all | solution.py:600
  60.8 0.0 copy-done
  60.8 0.0 copy-done.3
  60.8 2.4 %collect.2 = f32[16,8,128]{2,1,0:T(8,128)S(1)} custom-call(bf16[16,32,128]{2,1,0:T(8,128)(2,1)S(1)} %all_to_all.46.values, f32[2,128,128]{2,1,0:T(8,128)S(1)} %copy-done.3, bf16[16,8,128,128]{3,2,1,0:T(8,128)(2,1)S(1)} %copy-done), custom_call_target="tpu_custom_call" | custom-call | flops 33554432 | bytes 4194304 | tf_op jit(solution)/shard_map/collect/pallas_call | solution.py:666
  63.2 10.1 %all_to_all.47.terms = f32[16,8,128]{2,1,0:T(8,128)S(1)} all-to-all(f32[16,8,128]{2,1,0:T(8,128)S(1)} %collect.2), channel_id=1, replica_groups=mesh['grp'=2,'tm'=16] {'tm'}, dimensions={0} | all-to-all | bytes 131072 | tf_op jit(solution)/shard_map/all_to_all | solution.py:600
  73.2 0.7 sum_terms.2
  73.9 3.5 %all-to-all-start.4 = ((f32[16,8,128]{2,1,0:T(8,128)}), f32[16,8,128]{2,1,0:T(8,128)S(1)}, u32[]{:S(2)}, u32[]{:S(2)}) async-start(f32[16,8,128]{2,1,0:T(8,128)} %get-tuple-element.26), calls=%async_computation.4 | async-start | bytes 131072 | tf_op jit(solution)/shard_map/all_to_all | solution.py:600
  77.4 0.0 all-gather.5.cloned.1.call-start
  77.4 0.0 all-gather.3.cloned.1.call-done.gathered
  77.4 5.3 %flux_product.2 = (f32[1024,512]{1,0:T(8,128)}, f32[8,128]{1,0:T(8,128)S(1)}) custom-call(f32[8,128]{1,0:T(8,128)S(1)} %get-tuple-element.27.after, f32[136,2048]{1,0:T(8,128)} %get-tuple-element.28.parts, bf16[2048,512]{1,0:T(8,128)(2,1)} %all-gather.3.cloned.1.call-done.gathered), custom_call_target="tpu_custom_call" | custom-call | flops 2147483648 | bytes 2097152 | tf_op jit(solution)/shard_map/flux_product/pallas_call | solution.py:643
  82.8 1.4 all-to-all-done.4.image_in
  84.2 4.5 %update_spread.1 = (bf16[16,32,128]{2,1,0:T(8,128)(2,1)}, bf16[128,512]{1,0:T(8,128)(2,1)}, f32[16,8,128]{2,1,0:T(8,128)S(1)}, f32[16,128]{1,0:T(8,128)S(1)}, f32[16,128]{1,0:T(8,128)S(1)}) custom-call(f32[16,16,128]{2,1,0:T(8,128)S(1)} %all_to_all.45.everyone, f32[16,8,128]{2,1,0:T(8,128)S(1)} %all-to-all-done.4.image_in, f32[2,128,128]{2,1,0:T(8,128)S(1)} %copy-done.3, ...), custom_call_target="tpu_custom_call" | custom-call | flops 33554432 | bytes 4194304 | tf_op jit(solution)/shard_map/update_spread/pallas_call | solution.py:682
  88.8 0.0 all-gather.5.cloned.1.call-update
  88.8 4.6 %all-to-all-start.5 = ((bf16[16,32,128]{2,1,0:T(8,128)(2,1)}), bf16[16,32,128]{2,1,0:T(8,128)(2,1)S(1)}, u32[]{:S(2)}, u32[]{:S(2)}) async-start(bf16[16,32,128]{2,1,0:T(8,128)(2,1)} %get-tuple-element.31), calls=%async_computation.5 | async-start | bytes 262144 | tf_op jit(solution)/shard_map/all_to_all | solution.py:600
  93.4 2.6 %flux_first.1 = (f32[1024,512]{1,0:T(8,128)}, f32[8,128]{1,0:T(8,128)S(1)}) custom-call(f32[16,128]{1,0:T(8,128)S(1)} %get-tuple-element.32.sizes, f32[1024,512]{1,0:T(8,128)} %get-tuple-element.33.product), custom_call_target="tpu_custom_call" | custom-call | flops 16777216 | bytes 4194304 | tf_op jit(solution)/shard_map/flux_first/pallas_call | solution.py:692
  96.0 5.3 %all-to-all-done.5.columns = bf16[16,32,128]{2,1,0:T(8,128)(2,1)S(1)} async-done(((bf16[16,32,128]{2,1,0:T(8,128)(2,1)}), bf16[16,32,128]{2,1,0:T(8,128)(2,1)S(1)}, u32[]{:S(2)}, u32[]{:S(2)}) %all-to-all-start.5) | async-done | bytes 131104 | tf_op jit(solution)/shard_map/all_to_all | solution.py:600
  101.3 0.0 copy-start.1
  101.3 3.9 %mix_columns.3 = bf16[16,32,128]{2,1,0:T(8,128)(2,1)S(1)} custom-call(bf16[16,32,128]{2,1,0:T(8,128)(2,1)S(1)} %all-to-all-done.5.columns, bf16[2048,2048]{1,0:T(8,128)(2,1)} %get-tuple-element.25.tile_prior, f32[8,128]{1,0:T(8,128)S(1)} %get-tuple-element.34.rest_0_), custom_call_target="tpu_custom_call" | custom-call | flops 268435456 | bytes 8388608 | tf_op jit(solution)/shard_map/mix_columns/pallas_call | solution.py:654
  105.2 10.5 %all_to_all.48.values = bf16[16,32,128]{2,1,0:T(8,128)(2,1)S(1)} all-to-all(bf16[16,32,128]{2,1,0:T(8,128)(2,1)S(1)} %mix_columns.3), channel_id=1, replica_groups=mesh['grp'=2,'tm'=16] {'tm'}, dimensions={0} | all-to-all | bytes 262144 | tf_op jit(solution)/shard_map/all_to_all | solution.py:600
  115.8 0.0 copy-done.1
  115.8 2.4 %collect.3 = f32[16,8,128]{2,1,0:T(8,128)S(1)} custom-call(bf16[16,32,128]{2,1,0:T(8,128)(2,1)S(1)} %all_to_all.48.values, f32[2,128,128]{2,1,0:T(8,128)S(1)} %copy-done.3, bf16[16,8,128,128]{3,2,1,0:T(8,128)(2,1)S(1)} %copy-done.1), custom_call_target="tpu_custom_call" | custom-call | flops 33554432 | bytes 4194304 | tf_op jit(solution)/shard_map/collect/pallas_call | solution.py:666
  118.1 10.5 %all_to_all.49.terms = f32[16,8,128]{2,1,0:T(8,128)S(1)} all-to-all(f32[16,8,128]{2,1,0:T(8,128)S(1)} %collect.3), channel_id=1, replica_groups=mesh['grp'=2,'tm'=16] {'tm'}, dimensions={0} | all-to-all | bytes 131072 | tf_op jit(solution)/shard_map/all_to_all | solution.py:600
  128.6 0.7 sum_terms.3
  129.3 3.5 %all-to-all-start.8 = ((f32[16,8,128]{2,1,0:T(8,128)}), f32[16,8,128]{2,1,0:T(8,128)S(1)}, u32[]{:S(2)}, u32[]{:S(2)}) async-start(f32[16,8,128]{2,1,0:T(8,128)} %get-tuple-element.35), calls=%async_computation.8 | async-start | bytes 131072 | tf_op jit(solution)/shard_map/all_to_all | solution.py:600
  132.8 0.0 all-gather.5.cloned.1.call-done.gathered
  132.8 5.9 %flux_product.3 = (f32[1024,512]{1,0:T(8,128)}, f32[8,128]{1,0:T(8,128)}) custom-call(f32[8,128]{1,0:T(8,128)S(1)} %get-tuple-element.39.after, f32[136,2048]{1,0:T(8,128)} %get-tuple-element.28.parts, bf16[2048,512]{1,0:T(8,128)(2,1)} %all-gather.5.cloned.1.call-done.gathered), custom_call_target="tpu_custom_call" | custom-call | flops 2147483648 | bytes 2097152 | tf_op jit(solution)/shard_map/flux_product/pallas_call | solution.py:643
  138.8 0.9 all-to-all-done.8.image_in
  139.7 4.4 %last.1 = (f32[2,4,128]{2,1,0:T(4,128)}, f32[8,128,4,128]{3,2,1,0:T(4,128)}) custom-call(s32[1]{0:T(128)} %bitcast.me, f32[16,16,128]{2,1,0:T(8,128)S(1)} %all_to_all.45.everyone, f32[16,8,128]{2,1,0:T(8,128)S(1)} %all-to-all-done.8.image_in, f32[16,8,128]{2,1,0:T(8,128)S(1)} %get-tuple-element.36.direction, f32[16,128]{1,0:T(8,128)S(1)} %get-tuple-element.32.sizes, ...), custom_call_target="tpu_custom_call" | custom-call | flops 1048576 | bytes 6291456 | tf_op jit(solution)/shard_map/last/pallas_call | solution.py:705
Async XLA Ops:
  7.2 70.3 %all-gather.3.cloned.1.call-start = ((), (), s32[]{:S(2)}) async-start(), calls=%async_computation.9 | async-start | bytes 2228224 | tf_op jit(solution)/shard_map/all_gather | solution.py:622
  24.3 0.9 copy-start.2
  25.2 7.9 %copy-start.4 = (f32[128,128]{1,0:T(8,128)S(1)}, f32[128,128]{1,0:T(8,128)}, u32[]{:S(2)}) copy-start(f32[128,128]{1,0:T(8,128)} %time_cov.1) | copy-start | bytes 196612
  25.2 7.9 %copy-start.5 = (f32[128,128]{1,0:T(8,128)S(1)}, f32[128,128]{1,0:T(8,128)}, u32[]{:S(2)}) copy-start(f32[128,128]{1,0:T(8,128)} %lat_cov.1) | copy-start | bytes 196612
  29.6 11.6 %all-to-all-start.1 = ((bf16[16,32,128]{2,1,0:T(8,128)(2,1)}), bf16[16,32,128]{2,1,0:T(8,128)(2,1)S(1)}, u32[]{:S(2)}, u32[]{:S(2)}) async-start(bf16[16,32,128]{2,1,0:T(8,128)(2,1)} %get-tuple-element.24), calls=%async_computation.1 | async-start | bytes 262144 | tf_op jit(solution)/shard_map/all_to_all | solution.py:600
  41.2 19.6 %copy-start = (bf16[16,8,128,128]{3,2,1,0:T(8,128)(2,1)S(1)}, bf16[16,8,128,128]{3,2,1,0:T(8,128)(2,1)}, u32[]{:S(2)}) copy-start(bf16[16,8,128,128]{3,2,1,0:T(8,128)(2,1)} %footprint.7) | copy-start | bytes 12582916
  41.2 19.6 %copy-start.3 = (f32[2,128,128]{2,1,0:T(8,128)S(1)}, f32[2,128,128]{2,1,0:T(8,128)}, u32[]{:S(2)}) copy-start(f32[2,128,128]{2,1,0:T(8,128)} %get-tuple-element.23.mask_lon) | copy-start | bytes 393220
  73.9 10.4 %all-to-all-start.4 = ((f32[16,8,128]{2,1,0:T(8,128)}), f32[16,8,128]{2,1,0:T(8,128)S(1)}, u32[]{:S(2)}, u32[]{:S(2)}) async-start(f32[16,8,128]{2,1,0:T(8,128)} %get-tuple-element.26), calls=%async_computation.4 | async-start | bytes 131072 | tf_op jit(solution)/shard_map/all_to_all | solution.py:600
  77.4 55.5 %all-gather.5.cloned.1.call-start = ((), (), s32[]{:S(2)}) async-start(), calls=%async_computation.10 | async-start | bytes 2228224 | tf_op jit(solution)/shard_map/all_gather | solution.py:691
  88.8 12.5 %all-to-all-start.5 = ((bf16[16,32,128]{2,1,0:T(8,128)(2,1)}), bf16[16,32,128]{2,1,0:T(8,128)(2,1)S(1)}, u32[]{:S(2)}, u32[]{:S(2)}) async-start(bf16[16,32,128]{2,1,0:T(8,128)(2,1)} %get-tuple-element.31), calls=%async_computation.5 | async-start | bytes 262144 | tf_op jit(solution)/shard_map/all_to_all | solution.py:600
  101.3 14.5 %copy-start.1 = (bf16[16,8,128,128]{3,2,1,0:T(8,128)(2,1)S(1)}, bf16[16,8,128,128]{3,2,1,0:T(8,128)(2,1)}, u32[]{:S(2)}) copy-start(bf16[16,8,128,128]{3,2,1,0:T(8,128)(2,1)} %footprint.7) | copy-start | bytes 12582916
  129.3 10.4 %all-to-all-start.8 = ((f32[16,8,128]{2,1,0:T(8,128)}), f32[16,8,128]{2,1,0:T(8,128)S(1)}, u32[]{:S(2)}, u32[]{:S(2)}) async-start(f32[16,8,128]{2,1,0:T(8,128)} %get-tuple-element.35), calls=%async_computation.8 | async-start | bytes 131072 | tf_op jit(solution)/shard_map/all_to_all | solution.py:600
Sparse Core Ops, SparseCore 0:
  29.7 39.9 all-gather.2
  88.9 42.0 all-gather.4
where the time goes:
time: 152 us; the launch traced here: 151 us
  blocking collectives  62 us (41%)
  Pallas kernels  50.9 us (33%)
  starting transfers between devices  15.2 us (10%)
  between operations  14.2 us (9%)
  waiting for transfers between devices  7.73 us (5%)
    all_to_all x5, blocking collectives, exchange(): return lax.all_to_all(array, 'tm', split_axis=0, concat_axis=0, tiled=True)  62 us
    all_to_all x4, starting transfers between devices, exchange(): return lax.all_to_all(array, 'tm', split_axis=0, concat_axis=0, tiled=True)  15.1 us
    pallas_call x2, Pallas kernels, flux_product(): call(flux_product_body, [hbm, hbm, hbm], [hbm, vmem], [field_shape, token...  11.2 us
    pallas_call x1, Pallas kernels, by_columns(): call(build_body, [smem] + [vmem] * 3, [hbm, hbm], [prior_shape, parts_sha...  8.05 us
    pallas_call x2, Pallas kernels, prior(): call(mix_body, [vmem, hbm] + [hbm] * len(after), vmem, column_shape, [plt...  7.85 us
    all_to_all x4, waiting for transfers between devices, exchange(): return lax.all_to_all(array, 'tm', split_axis=0, concat_axis=0, tiled=True)  7.66 us
    pallas_call x2, Pallas kernels, collect(): call(collect_body, [vmem] * 3, vmem, vector_shape, [products], tile_cost,...  4.72 us
    pallas_call x1, Pallas kernels, by_columns(): call(update_body, [vmem] * 3 + [hbm] * 2, [vmem] * 5, [column_shape, tile...  4.54 us
  transfers between devices with their start and end apart: 6, of which 3 were waited for; matrix products, arithmetic and copies ran while one was open for 0% of the time, Pallas kernels for 24%

commit v1 on v0

--- a/solution.py
+++ b/solution.py
@@ -1,3 +1,5 @@
+import functools
+
 import jax
 import jax.numpy as jnp
 from jax import lax
@@ -230,7 +232,7 @@
     return jnp.sum(jnp.where(tile // slots == owner, rows, 0.0), axis=1, keepdims=True)
 
 
-def pack_body(right_sides, obs_var, tile_place, tile_block, lon, copies, mask_lon):
+def pack_body(right_sides, obs_var, tile_place, tile_block, lon, copies, mask, shelf, pair, sent):
     slots, owners = tile_place.shape
     tiles = owners * slots
     owner = lax.broadcasted_iota(jnp.int32, (owners, tiles), 0)
@@ -252,8 +254,13 @@
     copies[0, 11:16] = jnp.zeros((5, tiles), jnp.float32)
     for d in range(1, copies.shape[0]):
         copies[d] = copies[0]
-    mask_lon[0] = jnp.broadcast_to(second_of(tile_block), lon.shape)
-    mask_lon[1] = lon[...]
+    second = jnp.broadcast_to(second_of(tile_block), lon.shape)
+    mask[...] = second
+    pair[0] = second
+    pair[1] = lon[...]
+    shelve = pltpu.make_async_copy(pair, shelf.at[0:2], sent)
+    shelve.start()
+    shelve.wait()
 
 
 def spread_tiles(vectors, held, copies, products, split):
@@ -287,10 +294,14 @@
 
 
 def first_body(
-    everyone, mask_lon, footprint, by_column, by_tile, products, held, arrived
+    everyone, shelf, footprint,
+    by_column, by_tile, products, held, arrived, mask_lon, shelf_arrived,
 ):
     copies = fetch(footprint, held, arrived)
+    shelf_copy = pltpu.make_async_copy(shelf.at[0:2], mask_lon, shelf_arrived)
+    shelf_copy.start()
     spread_tiles(everyone, held, copies, products, False)
+    shelf_copy.wait()
     spread_end(products, mask_lon, by_column, by_tile)
 
 
@@ -312,11 +323,14 @@
 
 
 def update_body(
-    everyone, image_in, mask_lon, footprint, after,
-    by_column, by_tile, direction, sizes, norm, products, held, arrived,
+    everyone, image_in, shelf, footprint, after,
+    by_column, by_tile, direction, sizes, norm,
+    products, held, arrived, mask_lon, shelf_arrived,
 ):
     del after
     copies = fetch(footprint, held, arrived)
+    shelf_copy = pltpu.make_async_copy(shelf.at[0:2], mask_lon, shelf_arrived)
+    shelf_copy.start()
     first = everyone[:, 0:8, :]
     image = with_variance(image_in[...], everyone, first)
     norm_now = row_gram(first, first)
@@ -328,6 +342,7 @@
     keep(sizes, step_size)
     keep(norm, norm_next)
     spread_tiles(direction, held, copies, products, True)
+    shelf_copy.wait()
     spread_end(products, mask_lon, by_column, by_tile)
 
 
@@ -415,10 +430,10 @@
         copies[d] = value
 
 
-def collect_body(values, mask_lon, footprint, sums, rows):
+def collect_body(values, mask, footprint, sums, rows):
     chunks = values.shape[0] // SAMPLES
     owners, slots = footprint.shape[:2]
-    is_second = mask_lon[0] > 0.5
+    is_second = mask[...] > 0.5
     for k in range(SAMPLES):
         turned = values[k * chunks : (k + 1) * chunks].reshape(LON, -1)
         turned = turned.astype(jnp.float32).T
@@ -436,64 +451,86 @@
         sums[owner] = total
 
 
+def dense_rows(parts, first):
+    rows = []
+    for t in range(first, first + 2):
+        rows.append((parts[LAT + t : LAT + t + 1, :] * parts[:LAT]).astype(jnp.bfloat16))
+    return jnp.concatenate(rows, axis=0)
+
+
+def send_rows(ready, out, sent, step, value):
+    at = pl.ds(step * LAT, 2 * LAT)
+    ready[at] = value
+    copy = pltpu.make_async_copy(ready.at[at], out.at[at], sent.at[step // 2])
+    copy.start()
+    return copy
+
+
+def halved_product(dense, held, copies):
+    half = held.shape[0] // 2
+    total = 0.0
+    for h in range(2):
+        for copy in copies[h * PIECES // 2 : (h + 1) * PIECES // 2]:
+            copy.wait()
+        at = slice(h * half, (h + 1) * half)
+        total = total + jnp.dot(dense[:, at], held[at], preferred_element_type=jnp.float32)
+    return total
+
+
+def mixed_samples(value, size):
+    pieces = [value[:, k * LON : (k + 1) * LON] for k in range(SAMPLES)]
+    mixed = []
+    for j in range(SAMPLES):
+        mixed.append(sum(pieces[k] * size[k][j] for k in range(SAMPLES)))
+    return jnp.concatenate(mixed, axis=1)
+
+
 def flux_product_body(
-    after, parts, gathered, out, token,
+    rows, after, parts, gathered, out, token,
     ready, parts_held, held, parts_arrived, arrived, sent,
 ):
     del after
     (parts_copy,) = fetch(parts, parts_held, parts_arrived)
     copies = fetch(gathered, held, arrived)
-    steps = parts_held.shape[0] - LAT
-    half = held.shape[0] // 2
-    pair = 2
     parts_copy.wait()
     sending = []
-    for step in range(0, steps, pair):
-        dense = []
-        for t in range(step, step + pair):
-            times = parts_held[LAT + t : LAT + t + 1, :]
-            dense.append((times * parts_held[:LAT]).astype(jnp.bfloat16))
-        dense = jnp.concatenate(dense, axis=0)
-        at = pl.ds(step * LAT, pair * LAT)
+    for step in range(0, rows // LAT, 2):
+        dense = dense_rows(parts_held, step)
         if step == 0:
-            total = 0.0
-            for h in range(2):
-                for copy in copies[h * PIECES // 2 : (h + 1) * PIECES // 2]:
-                    copy.wait()
-                total = total + jnp.dot(
-                    dense[:, h * half : (h + 1) * half],
-                    held[h * half : (h + 1) * half],
-                    preferred_element_type=jnp.float32,
-                )
-            ready[at] = total
-            token[...] = ready[0:8, 0:128]
+            value = halved_product(dense, held, copies)
+            token[...] = value[0:8, 0:128]
         else:
-            ready[at] = jnp.dot(dense, held[...], preferred_element_type=jnp.float32)
-        copy = pltpu.make_async_copy(ready.at[at], out.at[at], sent.at[step // pair])
-        copy.start()
-        sending.append(copy)
+            value = jnp.dot(dense, held[...], preferred_element_type=jnp.float32)
+        sending.append(send_rows(ready, out, sent, step, value))
     for copy in sending:
         copy.wait()
 
 
-def flux_first_body(sizes, product, out, token, ready, held, arrived, sent):
-    copies = fetch(product, held, arrived)
+def flux_first_body(
+    sizes, product, parts, gathered, out, token,
+    ready, parts_held, held, parts_arrived, arrived, sent, product_held, product_arrived,
+):
+    done = product_held.shape[0] // LAT
+    product_copies = fetch(product.at[: done * LAT], product_held, product_arrived)
+    (parts_copy,) = fetch(parts, parts_held, parts_arrived)
+    copies = fetch(gathered, held, arrived)
     size = entries(sizes)
-    part = held.shape[0] // len(copies)
     sending = []
-    for p, copy in enumerate(copies):
+    for copy in product_copies:
         copy.wait()
-        at = pl.ds(p * part, part)
-        pieces = [held[at, k * LON : (k + 1) * LON] for k in range(SAMPLES)]
-        for j in range(SAMPLES):
-            value = 0.0
-            for k in range(SAMPLES):
-                value = value + pieces[k] * size[k][j]
-            ready[at, j * LON : (j + 1) * LON] = value
-        copy = pltpu.make_async_copy(ready.at[at], out.at[at], sent.at[p])
-        copy.start()
-        sending.append(copy)
-    token[...] = ready[0:8, 0:128]
+    for step in range(0, done, 2):
+        value = product_held[step * LAT : (step + 2) * LAT]
+        sending.append(send_rows(ready, out, sent, step, mixed_samples(value, size)))
+    parts_copy.wait()
+    for step in range(done, out.shape[0] // LAT, 2):
+        dense = dense_rows(parts_held, step)
+        if step == done:
+            value = halved_product(dense, held, copies)
+        else:
+            value = jnp.dot(dense, held[...], preferred_element_type=jnp.float32)
+        value = mixed_samples(value, size)
+        sending.append(send_rows(ready, out, sent, step, value))
+    token[...] = size[0][0] + jnp.zeros(token.shape, jnp.float32)
     for copy in sending:
         copy.wait()
 
@@ -578,7 +615,8 @@
     field = pltpu.VMEM(field_shape.shape, f32)
     gathered_held = pltpu.VMEM((every_tile, columns), bf16)
     prior_held = pltpu.VMEM(prior_shape.shape, bf16)
-    spread_scratch = [products, pltpu.VMEM(footprint.shape, bf16), flags(PIECES)]
+    spread_scratch = [products, pltpu.VMEM(footprint.shape, bf16), flags(2 * PIECES)]
+    spread_scratch += [pltpu.VMEM((2, 128, 128), f32), pltpu.SemaphoreType.DMA]
     flux_scratch = [field, pltpu.VMEM(parts_shape.shape, f32), gathered_held]
     flux_scratch += [flags(1), flags(PIECES), flags(steps_here // 2)]
     tile_cost = cost(2 * 8 * footprint.size, footprint.size * 2)
@@ -599,12 +637,17 @@
     def exchange(array):
         return lax.all_to_all(array, "tm", split_axis=0, concat_axis=0, tiled=True)
 
-    packed, mask_lon = call(
+    pair_scratch = [pltpu.VMEM((2, 128, 128), f32), pltpu.SemaphoreType.DMA]
+    packed, mask, shelf = call(
         pack_body,
         [vmem] * 5,
-        [vmem] * 2,
-        [shape_of((devices, 16, 128), f32), shape_of((2, 128, 128), f32)],
-        [],
+        [vmem, vmem, hbm],
+        [
+            shape_of((devices, 16, 128), f32),
+            shape_of((128, 128), f32),
+            shape_of((64, 128, 128), f32),
+        ],
+        pair_scratch,
         cost(0, 12 * MIB),
         "pack",
         59,
@@ -612,13 +655,13 @@
     everyone = exchange(packed)
     by_column, by_tile = call(
         first_body,
-        [vmem, vmem, hbm],
+        [vmem, hbm, hbm],
         [vmem] * 2,
         [column_shape, tile_shape],
         spread_scratch,
         tile_cost,
         "spread_first",
-    )(everyone, mask_lon, footprint)
+    )(everyone, shelf, footprint)
     gathered_one = lax.all_gather(by_tile, "tm", axis=0, tiled=True)
 
     tile_prior, parts = call(
@@ -639,9 +682,9 @@
         "build_prior",
     )(me, everyone, time_cov, lat_cov)
 
-    def flux_product(after, gathered):
+    def flux_product(after, gathered, rows):
         return call(
-            flux_product_body,
+            functools.partial(flux_product_body, rows),
             [hbm, hbm, hbm],
             [hbm, vmem],
             [field_shape, token_shape],
@@ -665,7 +708,7 @@
     def collect(values):
         sums = call(
             collect_body, [vmem] * 3, vmem, vector_shape, [products], tile_cost, "collect", 48
-        )(values, mask_lon, footprint)
+        )(values, mask, footprint)
         own, copies = call(
             sum_body,
             [vmem],
@@ -678,29 +721,29 @@
         return own, exchange(copies)
 
     own_image, image = collect(prior(by_column))
-    product_one, token = flux_product(own_image, gathered_one)
+    product_one, token = flux_product(own_image, gathered_one, rows_here // 2)
     by_column, by_tile, direction, sizes, norm = call(
         update_body,
-        [vmem] * 3 + [hbm] * 2,
+        [vmem] * 2 + [hbm] * 3,
         [vmem] * 5,
         [column_shape, tile_shape, vector_shape, small_shape, small_shape],
         spread_scratch,
         tile_cost,
         "update_spread",
-    )(everyone, image, mask_lon, footprint, token)
+    )(everyone, image, shelf, footprint, token)
     gathered_two = lax.all_gather(by_tile, "tm", axis=0, tiled=True)
     flux_one, token = call(
         flux_first_body,
-        [vmem, hbm],
+        [vmem, hbm, hbm, hbm],
         [hbm, vmem],
         [field_shape, token_shape],
-        [field, field, flags(4), flags(4)],
-        cost(1 << 24, 4 * MIB),
+        flux_scratch + [pltpu.VMEM((rows_here // 2, columns), f32), flags(2)],
+        flux_cost,
         "flux_first",
-    )(sizes, product_one)
+    )(sizes, product_one, parts, gathered_one)
 
     own_image, image = collect(prior(by_column, token))
-    flux_two, _ = flux_product(own_image, gathered_two)
+    flux_two, _ = flux_product(own_image, gathered_two, rows_here)
 
     answer, flux = call(
         last_body,

time: 152 us -> 153 us (level)
  Pallas kernels: 50.9 us -> 54.6 us
    pallas_call x6, Pallas kernels: 24.5 us -> 28.3 us  [the longest x2 10.2 us: flux_product(): call(functools.partial(flux_product_body, rows), [hbm, hbm, hbm], [hbm, v...]
where the time goes in v1:
time: 153 us; the launch traced here: 152 us
  blocking collectives  62.2 us (41%)
  Pallas kernels  54.6 us (36%)
  starting transfers between devices  14.3 us (9%)
  between operations  14.2 us (9%)
  waiting for transfers between devices  6.48 us (4%)
    all_to_all x5, blocking collectives, exchange(): return lax.all_to_all(array, 'tm', split_axis=0, concat_axis=0, tiled=True)  62.2 us
    all_to_all x4, starting transfers between devices, exchange(): return lax.all_to_all(array, 'tm', split_axis=0, concat_axis=0, tiled=True)  14.2 us
    pallas_call x2, Pallas kernels, flux_product(): call(functools.partial(flux_product_body, rows), [hbm, hbm, hbm], [hbm, v...  10.2 us
    pallas_call x1, Pallas kernels, by_columns(): call(build_body, [smem] + [vmem] * 3, [hbm, hbm], [prior_shape, parts_sha...  8.04 us
    pallas_call x2, Pallas kernels, prior(): call(mix_body, [vmem, hbm] + [hbm] * len(after), vmem, column_shape, [plt...  7.85 us
    all_to_all x4, waiting for transfers between devices, exchange(): return lax.all_to_all(array, 'tm', split_axis=0, concat_axis=0, tiled=True)  6.41 us
    pallas_call x1, Pallas kernels, by_columns(): call(first_body, [vmem, hbm, hbm], [vmem] * 2, [column_shape, tile_shape]...  5.47 us
    pallas_call x1, Pallas kernels, by_columns(): call(update_body, [vmem] * 2 + [hbm] * 3, [vmem] * 5, [column_shape, tile...  5.46 us
  transfers between devices with their start and end apart: 6, of which 3 were waited for; matrix products, arithmetic and copies ran while one was open for 0% of the time, Pallas kernels for 24%

profile of v1, /device:TPU:0, one launch (start us, length us, event | category | flops | bytes accessed | tf_op | source)
XLA Modules:
  0.0 151.8 jit_solution(16319465665754622722)
XLA Ops:
  7.2 0.0 all-gather.3.cloned.1.call-start
  7.2 2.5 %pack.1 = (f32[16,16,128]{2,1,0:T(8,128)}, f32[128,128]{1,0:T(8,128)}, f32[64,128,128]{2,1,0:T(8,128)}) custom-call(f32[2,4,128]{2,1,0:T(4,128)} %right_sides.1, f32[2,128]{1,0:T(2,128)} %obs_var.1, s32[8,16]{1,0:T(8,128)} %bitcast.3, s32[8,16]{1,0:T(8,128)} %bitcast.4, f32[128,128]{1,0:T(8,128)} %lon.1), custom_call_target="tpu_custom_call" | custom-call | bytes 12582912 | tf_op jit(solution)/shard_map/pack/pallas_call | solution.py:641
  9.7 15.3 %all_to_all.45.everyone = f32[16,16,128]{2,1,0:T(8,128)S(1)} all-to-all(f32[16,16,128]{2,1,0:T(8,128)} %get-tuple-element.23), channel_id=1, replica_groups=mesh['grp'=2,'tm'=16] {'tm'}, dimensions={0} | all-to-all | bytes 262144 | tf_op jit(solution)/shard_map/all_to_all | solution.py:638
  25.0 0.0 copy-start.3
  25.0 0.0 copy-start.4
  25.0 5.5 %spread_first.1 = (bf16[16,32,128]{2,1,0:T(8,128)(2,1)}, bf16[128,512]{1,0:T(8,128)(2,1)}) custom-call(f32[16,16,128]{2,1,0:T(8,128)S(1)} %all_to_all.45.everyone, f32[64,128,128]{2,1,0:T(8,128)} %get-tuple-element.24.shelf, bf16[16,8,128,128]{3,2,1,0:T(8,128)(2,1)} %footprint.7), custom_call_target="tpu_custom_call" | custom-call | flops 33554432 | bytes 4194304 | tf_op jit(solution)/shard_map/spread_first/pallas_call | solution.py:656
  30.5 0.0 all-gather.3.cloned.1.call-update
  30.5 3.5 %all-to-all-start.1 = ((bf16[16,32,128]{2,1,0:T(8,128)(2,1)}), bf16[16,32,128]{2,1,0:T(8,128)(2,1)S(1)}, u32[]{:S(2)}, u32[]{:S(2)}) async-start(bf16[16,32,128]{2,1,0:T(8,128)(2,1)} %get-tuple-element.25), calls=%async_computation.1 | async-start | bytes 262144 | tf_op jit(solution)/shard_map/all_to_all | solution.py:638
  34.0 0.0 copy-done.3
  34.1 0.0 copy-done.4
  34.1 8.0 %build_prior.1 = (bf16[2048,2048]{1,0:T(8,128)(2,1)}, f32[136,2048]{1,0:T(8,128)}) custom-call(s32[1]{0:T(128)} %bitcast.me, f32[16,16,128]{2,1,0:T(8,128)S(1)} %all_to_all.45.everyone, f32[128,128]{1,0:T(8,128)S(1)} %copy-done.3, f32[128,128]{1,0:T(8,128)S(1)} %copy-done.4), custom_call_target="tpu_custom_call" | custom-call | flops 4294967296 | bytes 8388608 | tf_op jit(solution)/shard_map/build_prior/pallas_call | solution.py:667
  42.1 0.0 all-to-all-done.1.columns
  42.1 0.0 copy-start
  42.1 0.0 copy-start.2
  42.1 3.9 %mix_columns.2 = bf16[16,32,128]{2,1,0:T(8,128)(2,1)S(1)} custom-call(bf16[16,32,128]{2,1,0:T(8,128)(2,1)S(1)} %all-to-all-done.1.columns, bf16[2048,2048]{1,0:T(8,128)(2,1)} %get-tuple-element.26.tile_prior), custom_call_target="tpu_custom_call" | custom-call | flops 268435456 | bytes 8388608 | tf_op jit(solution)/shard_map/mix_columns/pallas_call | solution.py:697
  46.1 15.6 %all_to_all.46.values = bf16[16,32,128]{2,1,0:T(8,128)(2,1)S(1)} all-to-all(bf16[16,32,128]{2,1,0:T(8,128)(2,1)S(1)} %mix_columns.2), channel_id=1, replica_groups=mesh['grp'=2,'tm'=16] {'tm'}, dimensions={0} | all-to-all | bytes 262144 | tf_op jit(solution)/shard_map/all_to_all | solution.py:638
  61.6 0.0 copy-done
  61.7 0.0 copy-done.2
  61.7 2.4 %collect.2 = f32[16,8,128]{2,1,0:T(8,128)S(1)} custom-call(bf16[16,32,128]{2,1,0:T(8,128)(2,1)S(1)} %all_to_all.46.values, f32[128,128]{1,0:T(8,128)S(1)} %copy-done.2, bf16[16,8,128,128]{3,2,1,0:T(8,128)(2,1)S(1)} %copy-done), custom_call_target="tpu_custom_call" | custom-call | flops 33554432 | bytes 4194304 | tf_op jit(solution)/shard_map/collect/pallas_call | solution.py:709
  64.0 10.1 %all_to_all.47.terms = f32[16,8,128]{2,1,0:T(8,128)S(1)} all-to-all(f32[16,8,128]{2,1,0:T(8,128)S(1)} %collect.2), channel_id=1, replica_groups=mesh['grp'=2,'tm'=16] {'tm'}, dimensions={0} | all-to-all | bytes 131072 | tf_op jit(solution)/shard_map/all_to_all | solution.py:638
  74.1 0.7 sum_terms.2
  74.8 3.5 %all-to-all-start.4 = ((f32[16,8,128]{2,1,0:T(8,128)}), f32[16,8,128]{2,1,0:T(8,128)S(1)}, u32[]{:S(2)}, u32[]{:S(2)}) async-start(f32[16,8,128]{2,1,0:T(8,128)} %get-tuple-element.28), calls=%async_computation.4 | async-start | bytes 131072 | tf_op jit(solution)/shard_map/all_to_all | solution.py:638
  78.3 0.0 all-gather.5.cloned.1.call-start
  78.3 0.0 all-gather.3.cloned.1.call-done.gathered
  78.3 4.2 %flux_product.2 = (f32[1024,512]{1,0:T(8,128)}, f32[8,128]{1,0:T(8,128)S(1)}) custom-call(f32[8,128]{1,0:T(8,128)S(1)} %get-tuple-element.29.after, f32[136,2048]{1,0:T(8,128)} %get-tuple-element.30.parts, bf16[2048,512]{1,0:T(8,128)(2,1)} %all-gather.3.cloned.1.call-done.gathered), custom_call_target="tpu_custom_call" | custom-call | flops 2147483648 | bytes 2097152 | tf_op jit(solution)/shard_map/flux_product/pallas_call | solution.py:686
  82.6 2.5 %all-to-all-done.4.image_in = f32[16,8,128]{2,1,0:T(8,128)S(1)} async-done(((f32[16,8,128]{2,1,0:T(8,128)}), f32[16,8,128]{2,1,0:T(8,128)S(1)}, u32[]{:S(2)}, u32[]{:S(2)}) %all-to-all-start.4) | async-done | bytes 65568 | tf_op jit(solution)/shard_map/all_to_all | solution.py:638
  85.1 5.5 %update_spread.1 = (bf16[16,32,128]{2,1,0:T(8,128)(2,1)}, bf16[128,512]{1,0:T(8,128)(2,1)}, f32[16,8,128]{2,1,0:T(8,128)S(1)}, f32[16,128]{1,0:T(8,128)S(1)}, f32[16,128]{1,0:T(8,128)S(1)}) custom-call(f32[16,16,128]{2,1,0:T(8,128)S(1)} %all_to_all.45.everyone, f32[16,8,128]{2,1,0:T(8,128)S(1)} %all-to-all-done.4.image_in, ...), custom_call_target="tpu_custom_call" | custom-call | flops 33554432 | bytes 4194304 | tf_op jit(solution)/shard_map/update_spread/pallas_call | solution.py:725
  90.6 0.0 all-gather.5.cloned.1.call-update
  90.6 3.7 %all-to-all-start.5 = ((bf16[16,32,128]{2,1,0:T(8,128)(2,1)}), bf16[16,32,128]{2,1,0:T(8,128)(2,1)S(1)}, u32[]{:S(2)}, u32[]{:S(2)}) async-start(bf16[16,32,128]{2,1,0:T(8,128)(2,1)} %get-tuple-element.33), calls=%async_computation.5 | async-start | bytes 262144 | tf_op jit(solution)/shard_map/all_to_all | solution.py:638
  94.3 4.8 %flux_first.1 = (f32[1024,512]{1,0:T(8,128)}, f32[8,128]{1,0:T(8,128)S(1)}) custom-call(f32[16,128]{1,0:T(8,128)S(1)} %get-tuple-element.34.sizes, f32[1024,512]{1,0:T(8,128)} %get-tuple-element.35.product, f32[136,2048]{1,0:T(8,128)} %get-tuple-element.30.parts, bf16[2048,512]{1,0:T(8,128)(2,1)} %all-gather.3.cloned.1.call-done.gathered), custom_call_target="tpu_custom_call" | custom-call | flops 2147483648 | bytes 2097152 | tf_op jit(solution)/shard_map/flux_first/pallas_call | solution.py:735
  99.1 3.0 %all-to-all-done.5.columns = bf16[16,32,128]{2,1,0:T(8,128)(2,1)S(1)} async-done(((bf16[16,32,128]{2,1,0:T(8,128)(2,1)}), bf16[16,32,128]{2,1,0:T(8,128)(2,1)S(1)}, u32[]{:S(2)}, u32[]{:S(2)}) %all-to-all-start.5) | async-done | bytes 131104 | tf_op jit(solution)/shard_map/all_to_all | solution.py:638
  102.0 0.0 copy-start.1
  102.0 3.9 %mix_columns.3 = bf16[16,32,128]{2,1,0:T(8,128)(2,1)S(1)} custom-call(bf16[16,32,128]{2,1,0:T(8,128)(2,1)S(1)} %all-to-all-done.5.columns, bf16[2048,2048]{1,0:T(8,128)(2,1)} %get-tuple-element.26.tile_prior, f32[8,128]{1,0:T(8,128)S(1)} %get-tuple-element.36.rest_0_), custom_call_target="tpu_custom_call" | custom-call | flops 268435456 | bytes 8388608 | tf_op jit(solution)/shard_map/mix_columns/pallas_call | solution.py:697
  106.0 10.7 %all_to_all.48.values = bf16[16,32,128]{2,1,0:T(8,128)(2,1)S(1)} all-to-all(bf16[16,32,128]{2,1,0:T(8,128)(2,1)S(1)} %mix_columns.3), channel_id=1, replica_groups=mesh['grp'=2,'tm'=16] {'tm'}, dimensions={0} | all-to-all | bytes 262144 | tf_op jit(solution)/shard_map/all_to_all | solution.py:638
  116.7 0.0 copy-done.1
  116.7 2.4 %collect.3 = f32[16,8,128]{2,1,0:T(8,128)S(1)} custom-call(bf16[16,32,128]{2,1,0:T(8,128)(2,1)S(1)} %all_to_all.48.values, f32[128,128]{1,0:T(8,128)S(1)} %copy-done.2, bf16[16,8,128,128]{3,2,1,0:T(8,128)(2,1)S(1)} %copy-done.1), custom_call_target="tpu_custom_call" | custom-call | flops 33554432 | bytes 4194304 | tf_op jit(solution)/shard_map/collect/pallas_call | solution.py:709
  119.0 10.5 %all_to_all.49.terms = f32[16,8,128]{2,1,0:T(8,128)S(1)} all-to-all(f32[16,8,128]{2,1,0:T(8,128)S(1)} %collect.3), channel_id=1, replica_groups=mesh['grp'=2,'tm'=16] {'tm'}, dimensions={0} | all-to-all | bytes 131072 | tf_op jit(solution)/shard_map/all_to_all | solution.py:638
  129.5 0.7 sum_terms.3
  130.2 3.5 %all-to-all-start.8 = ((f32[16,8,128]{2,1,0:T(8,128)}), f32[16,8,128]{2,1,0:T(8,128)S(1)}, u32[]{:S(2)}, u32[]{:S(2)}) async-start(f32[16,8,128]{2,1,0:T(8,128)} %get-tuple-element.37), calls=%async_computation.8 | async-start | bytes 131072 | tf_op jit(solution)/shard_map/all_to_all | solution.py:638
  133.7 0.0 all-gather.5.cloned.1.call-done.gathered
  133.7 5.9 %flux_product.3 = (f32[1024,512]{1,0:T(8,128)}, f32[8,128]{1,0:T(8,128)}) custom-call(f32[8,128]{1,0:T(8,128)S(1)} %get-tuple-element.41.after, f32[136,2048]{1,0:T(8,128)} %get-tuple-element.30.parts, bf16[2048,512]{1,0:T(8,128)(2,1)} %all-gather.5.cloned.1.call-done.gathered), custom_call_target="tpu_custom_call" | custom-call | flops 2147483648 | bytes 2097152 | tf_op jit(solution)/shard_map/flux_product/pallas_call | solution.py:686
  139.7 0.9 all-to-all-done.8.image_in
  140.6 4.4 %last.1 = (f32[2,4,128]{2,1,0:T(4,128)}, f32[8,128,4,128]{3,2,1,0:T(4,128)}) custom-call(s32[1]{0:T(128)} %bitcast.me, f32[16,16,128]{2,1,0:T(8,128)S(1)} %all_to_all.45.everyone, f32[16,8,128]{2,1,0:T(8,128)S(1)} %all-to-all-done.8.image_in, f32[16,8,128]{2,1,0:T(8,128)S(1)} %get-tuple-element.38.direction, f32[16,128]{1,0:T(8,128)S(1)} %get-tuple-element.34.sizes, ...), custom_call_target="tpu_custom_call" | custom-call | flops 1048576 | bytes 6291456 | tf_op jit(solution)/shard_map/last/pallas_call | solution.py:748
Async XLA Ops:
  7.2 71.2 %all-gather.3.cloned.1.call-start = ((), (), s32[]{:S(2)}) async-start(), calls=%async_computation.9 | async-start | bytes 2228224 | tf_op jit(solution)/shard_map/all_gather | solution.py:665
  25.0 9.0 %copy-start.3 = (f32[128,128]{1,0:T(8,128)S(1)}, f32[128,128]{1,0:T(8,128)}, u32[]{:S(2)}) copy-start(f32[128,128]{1,0:T(8,128)} %time_cov.1) | copy-start | bytes 196612
  25.0 9.0 %copy-start.4 = (f32[128,128]{1,0:T(8,128)S(1)}, f32[128,128]{1,0:T(8,128)}, u32[]{:S(2)}) copy-start(f32[128,128]{1,0:T(8,128)} %lat_cov.1) | copy-start | bytes 196612
  30.5 11.6 %all-to-all-start.1 = ((bf16[16,32,128]{2,1,0:T(8,128)(2,1)}), bf16[16,32,128]{2,1,0:T(8,128)(2,1)S(1)}, u32[]{:S(2)}, u32[]{:S(2)}) async-start(bf16[16,32,128]{2,1,0:T(8,128)(2,1)} %get-tuple-element.25), calls=%async_computation.1 | async-start | bytes 262144 | tf_op jit(solution)/shard_map/all_to_all | solution.py:638
  42.1 19.5 %copy-start = (bf16[16,8,128,128]{3,2,1,0:T(8,128)(2,1)S(1)}, bf16[16,8,128,128]{3,2,1,0:T(8,128)(2,1)}, u32[]{:S(2)}) copy-start(bf16[16,8,128,128]{3,2,1,0:T(8,128)(2,1)} %footprint.7) | copy-start | bytes 12582916
  42.1 19.5 %copy-start.2 = (f32[128,128]{1,0:T(8,128)S(1)}, f32[128,128]{1,0:T(8,128)}, u32[]{:S(2)}) copy-start(f32[128,128]{1,0:T(8,128)} %get-tuple-element.27.mask) | copy-start | bytes 196612
  74.8 10.4 %all-to-all-start.4 = ((f32[16,8,128]{2,1,0:T(8,128)}), f32[16,8,128]{2,1,0:T(8,128)S(1)}, u32[]{:S(2)}, u32[]{:S(2)}) async-start(f32[16,8,128]{2,1,0:T(8,128)} %get-tuple-element.28), calls=%async_computation.4 | async-start | bytes 131072 | tf_op jit(solution)/shard_map/all_to_all | solution.py:638
  78.3 55.5 %all-gather.5.cloned.1.call-start = ((), (), s32[]{:S(2)}) async-start(), calls=%async_computation.10 | async-start | bytes 2228224 | tf_op jit(solution)/shard_map/all_gather | solution.py:734
  90.6 11.4 %all-to-all-start.5 = ((bf16[16,32,128]{2,1,0:T(8,128)(2,1)}), bf16[16,32,128]{2,1,0:T(8,128)(2,1)S(1)}, u32[]{:S(2)}, u32[]{:S(2)}) async-start(bf16[16,32,128]{2,1,0:T(8,128)(2,1)} %get-tuple-element.33), calls=%async_computation.5 | async-start | bytes 262144 | tf_op jit(solution)/shard_map/all_to_all | solution.py:638
  102.0 14.6 %copy-start.1 = (bf16[16,8,128,128]{3,2,1,0:T(8,128)(2,1)S(1)}, bf16[16,8,128,128]{3,2,1,0:T(8,128)(2,1)}, u32[]{:S(2)}) copy-start(bf16[16,8,128,128]{3,2,1,0:T(8,128)(2,1)} %footprint.7) | copy-start | bytes 12582916
  130.2 10.4 %all-to-all-start.8 = ((f32[16,8,128]{2,1,0:T(8,128)}), f32[16,8,128]{2,1,0:T(8,128)S(1)}, u32[]{:S(2)}, u32[]{:S(2)}) async-start(f32[16,8,128]{2,1,0:T(8,128)} %get-tuple-element.37), calls=%async_computation.8 | async-start | bytes 131072 | tf_op jit(solution)/shard_map/all_to_all | solution.py:638
Sparse Core Ops, SparseCore 0:
  30.6 39.9 all-gather.2
  90.7 40.6 all-gather.4

commit v2 on v1

--- a/solution.py
+++ b/solution.py
@@ -297,9 +297,9 @@
     everyone, shelf, footprint,
     by_column, by_tile, products, held, arrived, mask_lon, shelf_arrived,
 ):
-    copies = fetch(footprint, held, arrived)
     shelf_copy = pltpu.make_async_copy(shelf.at[0:2], mask_lon, shelf_arrived)
     shelf_copy.start()
+    copies = fetch(footprint, held, arrived)
     spread_tiles(everyone, held, copies, products, False)
     shelf_copy.wait()
     spread_end(products, mask_lon, by_column, by_tile)
@@ -328,9 +328,9 @@
     products, held, arrived, mask_lon, shelf_arrived,
 ):
     del after
-    copies = fetch(footprint, held, arrived)
     shelf_copy = pltpu.make_async_copy(shelf.at[0:2], mask_lon, shelf_arrived)
     shelf_copy.start()
+    copies = fetch(footprint, held, arrived)
     first = everyone[:, 0:8, :]
     image = with_variance(image_in[...], everyone, first)
     norm_now = row_gram(first, first)
@@ -346,9 +346,16 @@
     spread_end(products, mask_lon, by_column, by_tile)
 
 
+def prior_rows(hot, cols, block):
+    by_time = jnp.dot(hot[0, block, :], cols[0], preferred_element_type=jnp.float32)
+    by_row = jnp.dot(hot[1, block, :], cols[1], preferred_element_type=jnp.float32)
+    return (by_time * by_row).astype(jnp.bfloat16)
+
+
 def build_body(
     me, everyone, time_cov, lat_cov,
-    prior_out, parts_out, tile_prior, hot, cols, times, parts, sent, parts_sent,
+    prior_out, parts_out, hot_out, cols_out,
+    tile_prior, hot, cols, times, parts, sent, rest_sent,
 ):
     devices, tiles = everyone.shape[0], everyone.shape[2]
     steps_here = parts.shape[0] - LAT
@@ -381,9 +388,16 @@
         else:
             parts[:LAT] = both
 
-    parts_copy = pltpu.make_async_copy(parts, parts_out, parts_sent)
-    parts_copy.start()
-    rows = tile_prior.shape[0] // PIECES
+    later = hot_out.shape[1]
+    rest = [
+        pltpu.make_async_copy(hot.at[:, later:], hot_out, rest_sent.at[0]),
+        pltpu.make_async_copy(cols, cols_out, rest_sent.at[1]),
+        pltpu.make_async_copy(parts, parts_out, rest_sent.at[2]),
+    ]
+    for copy in rest:
+        copy.start()
+    pieces = sent.shape[0]
+    rows = tile_prior.shape[0] // pieces
 
     def sending(piece):
         block = pl.ds(pl.multiple_of(piece * rows, rows), rows)
@@ -391,36 +405,74 @@
             tile_prior.at[block], prior_out.at[block], sent.at[piece]
         )
 
-    @pl.loop(0, PIECES)
+    @pl.loop(0, pieces)
     def _(piece):
         block = pl.ds(pl.multiple_of(piece * rows, rows), rows)
-        by_time = jnp.dot(hot[0, block, :], cols[0], preferred_element_type=jnp.float32)
-        by_row = jnp.dot(hot[1, block, :], cols[1], preferred_element_type=jnp.float32)
-        tile_prior[block, :] = (by_time * by_row).astype(jnp.bfloat16)
+        tile_prior[block, :] = prior_rows(hot, cols, block)
         sending(piece).start()
 
-    parts_copy.wait()
-    for piece in range(PIECES):
+    for copy in rest:
+        copy.wait()
+    for piece in range(pieces):
         sending(piece).wait()
 
 
-def mix_body(columns, tile_prior, *rest):
-    mixed, total, held, arrived = rest[-4:]
-    copies = fetch(tile_prior, held, arrived)
-    devices, width, tiles = columns.shape
-    part = devices // len(copies)
-    for p, copy in enumerate(copies):
-        at = range(p * part, (p + 1) * part)
-        lhs = jnp.concatenate([columns[d] for d in at], axis=1)
-        copy.wait()
-        product = jnp.dot(
-            lhs,
-            held[p * part * tiles : (p + 1) * part * tiles],
-            preferred_element_type=jnp.float32,
-        )
-        total[...] = product if p == 0 else total[...] + product
+def column_product(columns, first, block):
+    devices = block.shape[0] // columns.shape[2]
+    lhs = jnp.concatenate([columns[first + d] for d in range(devices)], axis=1)
+    return jnp.dot(lhs, block[...], preferred_element_type=jnp.float32)
+
+
+def split_columns(mixed, total):
+    devices, width, tiles = mixed.shape
     for d in range(devices):
         mixed[d] = total[:, d * tiles : (d + 1) * tiles].astype(jnp.bfloat16)
+
+
+def build_mix_body(
+    columns, hot_in, cols_in, prior_one,
+    mixed, prior_two, total, hot, cols, held, built, hot_arrived, arrived, sent,
+):
+    cols_copies = fetch(cols_in, cols, hot_arrived.at[0:1])
+    hot_copies = fetch(hot_in, hot, hot_arrived.at[1:2])
+    copies = fetch(prior_one, held, arrived)
+    half = columns.shape[0] // 2
+    pieces = len(copies)
+    rows = built.shape[0] // pieces
+    for copy in cols_copies + hot_copies:
+        copy.wait()
+    sending = []
+    for p in range(pieces):
+        block = pl.ds(p * rows, rows)
+        built[block, :] = prior_rows(hot, cols, block)
+        copy = pltpu.make_async_copy(built.at[block], prior_two.at[block], sent.at[p])
+        copy.start()
+        sending.append(copy)
+        first = half + p * half // pieces
+        product = column_product(columns, first, built.at[block])
+        total[...] = product if p == 0 else total[...] + product
+    for p, copy in enumerate(copies):
+        copy.wait()
+        block = pl.ds(p * rows, rows)
+        total[...] += column_product(columns, p * half // pieces, held.at[block])
+    split_columns(mixed, total)
+    for copy in sending:
+        copy.wait()
+
+
+def mix_body(columns, prior_one, prior_two, *rest):
+    mixed, total, held_one, held_two, arrived_one, arrived_two = rest[-6:]
+    one = fetch(prior_one, held_one, arrived_one)
+    two = fetch(prior_two, held_two, arrived_two)
+    half = columns.shape[0] // 2
+    rows = held_one.shape[0] // len(one)
+    for first, held, copies in ((0, held_one, one), (half, held_two, two)):
+        for p, copy in enumerate(copies):
+            copy.wait()
+            at = first + p * half // len(copies)
+            product = column_product(columns, at, held.at[pl.ds(p * rows, rows)])
+            total[...] = product if at == 0 else total[...] + product
+    split_columns(mixed, total)
 
 
 def sum_body(terms, total, copies):
@@ -605,7 +657,7 @@
     field_shape = shape_of((rows_here, columns), f32)
     parts_shape = shape_of((LAT + steps_here, every_tile), f32)
     token_shape = shape_of((8, 128), f32)
-    prior_shape = shape_of((every_tile, every_tile), bf16)
+    prior_shape = shape_of((every_tile // 2, every_tile), bf16)
     flux_shape = shape_of((steps_here, LAT, SAMPLES, LON), f32)
 
     def flags(count):
@@ -615,7 +667,7 @@
     field = pltpu.VMEM(field_shape.shape, f32)
     gathered_held = pltpu.VMEM((every_tile, columns), bf16)
     prior_held = pltpu.VMEM(prior_shape.shape, bf16)
-    spread_scratch = [products, pltpu.VMEM(footprint.shape, bf16), flags(2 * PIECES)]
+    spread_scratch = [products, pltpu.VMEM(footprint.shape, bf16), flags(4)]
     spread_scratch += [pltpu.VMEM((2, 128, 128), f32), pltpu.SemaphoreType.DMA]
     flux_scratch = [field, pltpu.VMEM(parts_shape.shape, f32), gathered_held]
     flux_scratch += [flags(1), flags(PIECES), flags(steps_here // 2)]
@@ -664,21 +716,23 @@
     )(everyone, shelf, footprint)
     gathered_one = lax.all_gather(by_tile, "tm", axis=0, tiled=True)
 
-    tile_prior, parts = call(
+    hot_shape = shape_of((2, every_tile // 2, 2 * LAT), bf16)
+    cols_shape = shape_of((2, 2 * LAT, every_tile), bf16)
+    prior_one, parts, hot, cols = call(
         build_body,
         [smem] + [vmem] * 3,
-        [hbm, hbm],
-        [prior_shape, parts_shape],
+        [hbm] * 4,
+        [prior_shape, parts_shape, hot_shape, cols_shape],
         [
             prior_held,
             pltpu.VMEM((2, every_tile, 2 * LAT), bf16),
-            pltpu.VMEM((2, 2 * LAT, every_tile), bf16),
+            pltpu.VMEM(cols_shape.shape, bf16),
             pltpu.VMEM((LAT, every_tile), f32),
             pltpu.VMEM(parts_shape.shape, f32),
-            flags(PIECES),
-            pltpu.SemaphoreType.DMA,
+            flags(4),
+            flags(3),
         ],
-        cost(4 * every_tile * every_tile * 256, every_tile * every_tile * 2),
+        cost(2 * every_tile * every_tile * 256, every_tile * every_tile * 2),
         "build_prior",
     )(me, everyone, time_cov, lat_cov)
 
@@ -693,17 +747,37 @@
             "flux_product",
         )(after, parts, gathered)
 
-    def prior(by_column, *after):
-        mixed = call(
+    mix_total = pltpu.VMEM((width, every_tile), f32)
+    mix_cost = cost(2 * width * every_tile**2, every_tile**2 * 2)
+    mixed, prior_two = call(
+        build_mix_body,
+        [vmem] + [hbm] * 3,
+        [vmem, hbm],
+        [column_shape, prior_shape],
+        [
+            mix_total,
+            pltpu.VMEM(hot_shape.shape, bf16),
+            pltpu.VMEM(cols_shape.shape, bf16),
+            prior_held,
+            prior_held,
+            flags(2),
+            flags(4),
+            flags(4),
+        ],
+        mix_cost,
+        "build_mix",
+    )(exchange(by_column), hot, cols, prior_one)
+
+    def mix(by_column, after):
+        return call(
             mix_body,
-            [vmem, hbm] + [hbm] * len(after),
+            [vmem] + [hbm] * 3,
             vmem,
             column_shape,
-            [pltpu.VMEM((width, every_tile), f32), prior_held, flags(PIECES)],
-            cost(2 * width * every_tile**2, every_tile**2 * 2),
+            [mix_total, prior_held, prior_held, flags(4), flags(4)],
+            mix_cost,
             "mix_columns",
-        )(exchange(by_column), tile_prior, *after)
-        return exchange(mixed)
+        )(exchange(by_column), prior_one, prior_two, after)
 
     def collect(values):
         sums = call(
@@ -720,7 +794,7 @@
         )(exchange(sums))
         return own, exchange(copies)
 
-    own_image, image = collect(prior(by_column))
+    own_image, image = collect(exchange(mixed))
     product_one, token = flux_product(own_image, gathered_one, rows_here // 2)
     by_column, by_tile, direction, sizes, norm = call(
         update_body,
@@ -742,7 +816,7 @@
         "flux_first",
     )(sizes, product_one, parts, gathered_one)
 
-    own_image, image = collect(prior(by_column, token))
+    own_image, image = collect(exchange(mix(by_column, token)))
     flux_two, _ = flux_product(own_image, gathered_two, rows_here)
 
     answer, flux = call(

time: 153 us -> 152 us (level)
  waiting for transfers between devices: 6.48 us -> 9.38 us
  blocking collectives: 62.2 us -> 60.5 us
    all_to_all x4, waiting for transfers between devices: 6.41 us -> 9.31 us  [exchange(): return lax.all_to_all(array, 'tm', split_axis=0, concat_axis=0, tiled=True)]
    all_to_all x5, blocking collectives: 62.2 us -> 60.5 us  [exchange(): return lax.all_to_all(array, 'tm', split_axis=0, concat_axis=0, tiled=True)]
  transfers between devices with their start and end apart: 6 -> 6, of which waited for: 3 -> 4; matrix products, arithmetic and copies ran while one was open for 0% -> 0% of each run, Pallas kernels for 24% -> 25%
where the time goes in v2:
time: 152 us
  blocking collectives  60.5 us (40%)
  Pallas kernels  53.1 us (35%)
  starting transfers between devices  14.4 us (9%)
  between operations  14.2 us (9%)
  waiting for transfers between devices  9.38 us (6%)
    all_to_all x5, blocking collectives, exchange(): return lax.all_to_all(array, 'tm', split_axis=0, concat_axis=0, tiled=True)  60.5 us
    all_to_all x4, starting transfers between devices, exchange(): return lax.all_to_all(array, 'tm', split_axis=0, concat_axis=0, tiled=True)  14.2 us
    pallas_call x2, Pallas kernels, flux_product(): call(functools.partial(flux_product_body, rows), [hbm, hbm, hbm], [hbm, v...  10.2 us
    all_to_all x4, waiting for transfers between devices, exchange(): return lax.all_to_all(array, 'tm', split_axis=0, concat_axis=0, tiled=True)  9.31 us
    pallas_call x1, Pallas kernels, by_columns(): call(build_mix_body, [vmem] + [hbm] * 3, [vmem, hbm], [column_shape, prio...  7.04 us
    pallas_call x1, Pallas kernels, by_columns(): call(build_body, [smem] + [vmem] * 3, [hbm] * 4, [prior_shape, parts_shap...  5.15 us
    pallas_call x2, Pallas kernels, collect(): call(collect_body, [vmem] * 3, vmem, vector_shape, [products], tile_cost,...  4.72 us
    pallas_call x1, Pallas kernels, by_columns(): call(flux_first_body, [vmem, hbm, hbm, hbm], [hbm, vmem], [field_shape, t...  4.72 us
  transfers between devices with their start and end apart: 6, of which 4 were waited for; matrix products, arithmetic and copies ran while one was open for 0% of the time, Pallas kernels for 25%

profile of v2, /device:TPU:0, one launch (start us, length us, event | category | flops | bytes accessed | tf_op | source)
XLA Modules:
  0.0 151.6 jit_solution(6627097934784823353)
XLA Ops:
  7.2 0.0 all-gather.3.cloned.1.call-start
  7.2 2.4 %pack.1 = (f32[16,16,128]{2,1,0:T(8,128)}, f32[128,128]{1,0:T(8,128)}, f32[64,128,128]{2,1,0:T(8,128)}) custom-call(f32[2,4,128]{2,1,0:T(4,128)} %right_sides.1, f32[2,128]{1,0:T(2,128)} %obs_var.1, s32[8,16]{1,0:T(8,128)} %bitcast.3, s32[8,16]{1,0:T(8,128)} %bitcast.4, f32[128,128]{1,0:T(8,128)} %lon.1), custom_call_target="tpu_custom_call" | custom-call | bytes 12582912 | tf_op jit(solution)/shard_map/pack/pallas_call | solution.py:693
  9.7 15.3 %all_to_all.45.everyone = f32[16,16,128]{2,1,0:T(8,128)S(1)} all-to-all(f32[16,16,128]{2,1,0:T(8,128)} %get-tuple-element.27), channel_id=1, replica_groups=mesh['grp'=2,'tm'=16] {'tm'}, dimensions={0} | all-to-all | bytes 262144 | tf_op jit(solution)/shard_map/all_to_all | solution.py:690
  25.0 0.0 copy-start.3
  25.0 0.0 copy-start.4
  25.0 4.3 %spread_first.1 = (bf16[16,32,128]{2,1,0:T(8,128)(2,1)}, bf16[128,512]{1,0:T(8,128)(2,1)}) custom-call(f32[16,16,128]{2,1,0:T(8,128)S(1)} %all_to_all.45.everyone, f32[64,128,128]{2,1,0:T(8,128)} %get-tuple-element.28.shelf, bf16[16,8,128,128]{3,2,1,0:T(8,128)(2,1)} %footprint.7), custom_call_target="tpu_custom_call" | custom-call | flops 33554432 | bytes 4194304 | tf_op jit(solution)/shard_map/spread_first/pallas_call | solution.py:708
  29.3 0.0 all-gather.3.cloned.1.call-update
  29.3 3.5 %all-to-all-start.1 = ((bf16[16,32,128]{2,1,0:T(8,128)(2,1)}), bf16[16,32,128]{2,1,0:T(8,128)(2,1)S(1)}, u32[]{:S(2)}, u32[]{:S(2)}) async-start(bf16[16,32,128]{2,1,0:T(8,128)(2,1)} %get-tuple-element.29), calls=%async_computation.1 | async-start | bytes 262144 | tf_op jit(solution)/shard_map/all_to_all | solution.py:690
  32.8 0.0 copy-done.3
  32.8 0.0 copy-done.4
  32.8 5.2 %build_prior.1 = (bf16[1024,2048]{1,0:T(8,128)(2,1)}, f32[136,2048]{1,0:T(8,128)}, bf16[2,1024,256]{2,1,0:T(8,128)(2,1)}, bf16[2,256,2048]{2,1,0:T(8,128)(2,1)}) custom-call(s32[1]{0:T(128)} %bitcast.me, f32[16,16,128]{2,1,0:T(8,128)S(1)} %all_to_all.45.everyone, f32[128,128]{1,0:T(8,128)S(1)} %copy-done.3, f32[128,128]{1,0:T(8,128)S(1)} %copy-done.4), custom_call_target="tpu_custom_call" | custom-call | flops 2147483648 | bytes 8388608 | tf_op jit(solution)/shard_map/build_prior/pallas_call | solution.py:721
  38.0 2.9 %all-to-all-done.1.columns = bf16[16,32,128]{2,1,0:T(8,128)(2,1)S(1)} async-done(((bf16[16,32,128]{2,1,0:T(8,128)(2,1)}), bf16[16,32,128]{2,1,0:T(8,128)(2,1)S(1)}, u32[]{:S(2)}, u32[]{:S(2)}) %all-to-all-start.1) | async-done | bytes 131104 | tf_op jit(solution)/shard_map/all_to_all | solution.py:690
  40.9 0.0 copy-start
  40.9 0.0 copy-start.2
  40.9 7.0 %build_mix.1 = (bf16[16,32,128]{2,1,0:T(8,128)(2,1)S(1)}, bf16[1024,2048]{1,0:T(8,128)(2,1)}) custom-call(bf16[16,32,128]{2,1,0:T(8,128)(2,1)S(1)} %all-to-all-done.1.columns, bf16[2,1024,256]{2,1,0:T(8,128)(2,1)} %get-tuple-element.30.hot_in, bf16[2,256,2048]{2,1,0:T(8,128)(2,1)} %get-tuple-element.31.cols_in, bf16[1024,2048]{1,0:T(8,128)(2,1)} %get-tuple-element.32.prior_one), custom_call_target="tpu_custom_call" | custom-call | flops 268435456 | bytes 8388608 | tf_op jit(solution)/shard_map/build_mix/pallas_call | solution.py:752
  47.9 13.5 %all_to_all.46.values = bf16[16,32,128]{2,1,0:T(8,128)(2,1)S(1)} all-to-all(bf16[16,32,128]{2,1,0:T(8,128)(2,1)S(1)} %get-tuple-element.33), channel_id=1, replica_groups=mesh['grp'=2,'tm'=16] {'tm'}, dimensions={0} | all-to-all | bytes 262144 | tf_op jit(solution)/shard_map/all_to_all | solution.py:690
  61.4 0.0 copy-done
  61.4 0.0 copy-done.2
  61.4 2.4 %collect.2 = f32[16,8,128]{2,1,0:T(8,128)S(1)} custom-call(bf16[16,32,128]{2,1,0:T(8,128)(2,1)S(1)} %all_to_all.46.values, f32[128,128]{1,0:T(8,128)S(1)} %copy-done.2, bf16[16,8,128,128]{3,2,1,0:T(8,128)(2,1)S(1)} %copy-done), custom_call_target="tpu_custom_call" | custom-call | flops 33554432 | bytes 4194304 | tf_op jit(solution)/shard_map/collect/pallas_call | solution.py:783
  63.8 10.5 %all_to_all.47.terms = f32[16,8,128]{2,1,0:T(8,128)S(1)} all-to-all(f32[16,8,128]{2,1,0:T(8,128)S(1)} %collect.2), channel_id=1, replica_groups=mesh['grp'=2,'tm'=16] {'tm'}, dimensions={0} | all-to-all | bytes 131072 | tf_op jit(solution)/shard_map/all_to_all | solution.py:690
  74.3 0.6 sum_terms.2
  75.0 3.5 %all-to-all-start.4 = ((f32[16,8,128]{2,1,0:T(8,128)}), f32[16,8,128]{2,1,0:T(8,128)S(1)}, u32[]{:S(2)}, u32[]{:S(2)}) async-start(f32[16,8,128]{2,1,0:T(8,128)} %get-tuple-element.35), calls=%async_computation.4 | async-start | bytes 131072 | tf_op jit(solution)/shard_map/all_to_all | solution.py:690
  78.5 0.2 all-gather.5.cloned.1.call-start
  78.7 0.0 all-gather.3.cloned.1.call-done.gathered
  78.7 4.2 %flux_product.2 = (f32[1024,512]{1,0:T(8,128)}, f32[8,128]{1,0:T(8,128)S(1)}) custom-call(f32[8,128]{1,0:T(8,128)S(1)} %get-tuple-element.36.after, f32[136,2048]{1,0:T(8,128)} %get-tuple-element.37.parts, bf16[2048,512]{1,0:T(8,128)(2,1)} %all-gather.3.cloned.1.call-done.gathered), custom_call_target="tpu_custom_call" | custom-call | flops 2147483648 | bytes 2097152 | tf_op jit(solution)/shard_map/flux_product/pallas_call | solution.py:740
  83.0 2.3 %all-to-all-done.4.image_in = f32[16,8,128]{2,1,0:T(8,128)S(1)} async-done(((f32[16,8,128]{2,1,0:T(8,128)}), f32[16,8,128]{2,1,0:T(8,128)S(1)}, u32[]{:S(2)}, u32[]{:S(2)}) %all-to-all-start.4) | async-done | bytes 65568 | tf_op jit(solution)/shard_map/all_to_all | solution.py:690
  85.3 4.4 %update_spread.1 = (bf16[16,32,128]{2,1,0:T(8,128)(2,1)}, bf16[128,512]{1,0:T(8,128)(2,1)}, f32[16,8,128]{2,1,0:T(8,128)S(1)}, f32[16,128]{1,0:T(8,128)S(1)}, f32[16,128]{1,0:T(8,128)S(1)}) custom-call(f32[16,16,128]{2,1,0:T(8,128)S(1)} %all_to_all.45.everyone, f32[16,8,128]{2,1,0:T(8,128)S(1)} %all-to-all-done.4.image_in, ...), custom_call_target="tpu_custom_call" | custom-call | flops 33554432 | bytes 4194304 | tf_op jit(solution)/shard_map/update_spread/pallas_call | solution.py:799
  89.7 0.0 all-gather.5.cloned.1.call-update
  89.8 3.6 %all-to-all-start.5 = ((bf16[16,32,128]{2,1,0:T(8,128)(2,1)}), bf16[16,32,128]{2,1,0:T(8,128)(2,1)S(1)}, u32[]{:S(2)}, u32[]{:S(2)}) async-start(bf16[16,32,128]{2,1,0:T(8,128)(2,1)} %get-tuple-element.40), calls=%async_computation.5 | async-start | bytes 262144 | tf_op jit(solution)/shard_map/all_to_all | solution.py:690
  93.4 4.7 %flux_first.1 = (f32[1024,512]{1,0:T(8,128)}, f32[8,128]{1,0:T(8,128)S(1)}) custom-call(f32[16,128]{1,0:T(8,128)S(1)} %get-tuple-element.42.sizes, f32[1024,512]{1,0:T(8,128)} %get-tuple-element.43.product, f32[136,2048]{1,0:T(8,128)} %get-tuple-element.37.parts, bf16[2048,512]{1,0:T(8,128)(2,1)} %all-gather.3.cloned.1.call-done.gathered), custom_call_target="tpu_custom_call" | custom-call | flops 2147483648 | bytes 2097152 | tf_op jit(solution)/shard_map/flux_first/pallas_call | solution.py:809
  98.2 3.2 %all-to-all-done.5.columns = bf16[16,32,128]{2,1,0:T(8,128)(2,1)S(1)} async-done(((bf16[16,32,128]{2,1,0:T(8,128)(2,1)}), bf16[16,32,128]{2,1,0:T(8,128)(2,1)S(1)}, u32[]{:S(2)}, u32[]{:S(2)}) %all-to-all-start.5) | async-done | bytes 131104 | tf_op jit(solution)/shard_map/all_to_all | solution.py:690
  101.4 0.0 copy-start.1
  101.4 4.4 %mix_columns.1 = bf16[16,32,128]{2,1,0:T(8,128)(2,1)S(1)} custom-call(bf16[16,32,128]{2,1,0:T(8,128)(2,1)S(1)} %all-to-all-done.5.columns, bf16[1024,2048]{1,0:T(8,128)(2,1)} %get-tuple-element.32.prior_one, bf16[1024,2048]{1,0:T(8,128)(2,1)} %get-tuple-element.41.prior_two, f32[8,128]{1,0:T(8,128)S(1)} %get-tuple-element.44.rest_0_), custom_call_target="tpu_custom_call" | custom-call | flops 268435456 | bytes 8388608 | tf_op jit(solution)/shard_map/mix_columns/pallas_call | solution.py:772
  105.8 10.7 %all_to_all.48.values = bf16[16,32,128]{2,1,0:T(8,128)(2,1)S(1)} all-to-all(bf16[16,32,128]{2,1,0:T(8,128)(2,1)S(1)} %mix_columns.1), channel_id=1, replica_groups=mesh['grp'=2,'tm'=16] {'tm'}, dimensions={0} | all-to-all | bytes 262144 | tf_op jit(solution)/shard_map/all_to_all | solution.py:690
  116.4 0.0 copy-done.1
  116.4 2.4 %collect.3 = f32[16,8,128]{2,1,0:T(8,128)S(1)} custom-call(bf16[16,32,128]{2,1,0:T(8,128)(2,1)S(1)} %all_to_all.48.values, f32[128,128]{1,0:T(8,128)S(1)} %copy-done.2, bf16[16,8,128,128]{3,2,1,0:T(8,128)(2,1)S(1)} %copy-done.1), custom_call_target="tpu_custom_call" | custom-call | flops 33554432 | bytes 4194304 | tf_op jit(solution)/shard_map/collect/pallas_call | solution.py:783
  118.8 10.5 %all_to_all.49.terms = f32[16,8,128]{2,1,0:T(8,128)S(1)} all-to-all(f32[16,8,128]{2,1,0:T(8,128)S(1)} %collect.3), channel_id=1, replica_groups=mesh['grp'=2,'tm'=16] {'tm'}, dimensions={0} | all-to-all | bytes 131072 | tf_op jit(solution)/shard_map/all_to_all | solution.py:690
  129.3 0.7 sum_terms.3
  130.0 3.5 %all-to-all-start.8 = ((f32[16,8,128]{2,1,0:T(8,128)}), f32[16,8,128]{2,1,0:T(8,128)S(1)}, u32[]{:S(2)}, u32[]{:S(2)}) async-start(f32[16,8,128]{2,1,0:T(8,128)} %get-tuple-element.45), calls=%async_computation.8 | async-start | bytes 131072 | tf_op jit(solution)/shard_map/all_to_all | solution.py:690
  133.5 0.0 all-gather.5.cloned.1.call-done.gathered
  133.5 5.9 %flux_product.3 = (f32[1024,512]{1,0:T(8,128)}, f32[8,128]{1,0:T(8,128)}) custom-call(f32[8,128]{1,0:T(8,128)S(1)} %get-tuple-element.49.after, f32[136,2048]{1,0:T(8,128)} %get-tuple-element.37.parts, bf16[2048,512]{1,0:T(8,128)(2,1)} %all-gather.5.cloned.1.call-done.gathered), custom_call_target="tpu_custom_call" | custom-call | flops 2147483648 | bytes 2097152 | tf_op jit(solution)/shard_map/flux_product/pallas_call | solution.py:740
  139.4 0.9 all-to-all-done.8.image_in
  140.3 4.4 %last.1 = (f32[2,4,128]{2,1,0:T(4,128)}, f32[8,128,4,128]{3,2,1,0:T(4,128)}) custom-call(s32[1]{0:T(128)} %bitcast.me, f32[16,16,128]{2,1,0:T(8,128)S(1)} %all_to_all.45.everyone, f32[16,8,128]{2,1,0:T(8,128)S(1)} %all-to-all-done.8.image_in, f32[16,8,128]{2,1,0:T(8,128)S(1)} %get-tuple-element.46.direction, f32[16,128]{1,0:T(8,128)S(1)} %get-tuple-element.42.sizes, ...), custom_call_target="tpu_custom_call" | custom-call | flops 1048576 | bytes 6291456 | tf_op jit(solution)/shard_map/last/pallas_call | solution.py:822
Async XLA Ops:
  7.2 71.5 %all-gather.3.cloned.1.call-start = ((), (), s32[]{:S(2)}) async-start(), calls=%async_computation.9 | async-start | bytes 2228224 | tf_op jit(solution)/shard_map/all_gather | solution.py:717
  25.0 7.8 %copy-start.3 = (f32[128,128]{1,0:T(8,128)S(1)}, f32[128,128]{1,0:T(8,128)}, u32[]{:S(2)}) copy-start(f32[128,128]{1,0:T(8,128)} %time_cov.1) | copy-start | bytes 196612
  25.0 7.8 %copy-start.4 = (f32[128,128]{1,0:T(8,128)S(1)}, f32[128,128]{1,0:T(8,128)}, u32[]{:S(2)}) copy-start(f32[128,128]{1,0:T(8,128)} %lat_cov.1) | copy-start | bytes 196612
  29.3 11.6 %all-to-all-start.1 = ((bf16[16,32,128]{2,1,0:T(8,128)(2,1)}), bf16[16,32,128]{2,1,0:T(8,128)(2,1)S(1)}, u32[]{:S(2)}, u32[]{:S(2)}) async-start(bf16[16,32,128]{2,1,0:T(8,128)(2,1)} %get-tuple-element.29), calls=%async_computation.1 | async-start | bytes 262144 | tf_op jit(solution)/shard_map/all_to_all | solution.py:690
  40.9 20.6 %copy-start = (bf16[16,8,128,128]{3,2,1,0:T(8,128)(2,1)S(1)}, bf16[16,8,128,128]{3,2,1,0:T(8,128)(2,1)}, u32[]{:S(2)}) copy-start(bf16[16,8,128,128]{3,2,1,0:T(8,128)(2,1)} %footprint.7) | copy-start | bytes 12582916
  40.9 20.6 %copy-start.2 = (f32[128,128]{1,0:T(8,128)S(1)}, f32[128,128]{1,0:T(8,128)}, u32[]{:S(2)}) copy-start(f32[128,128]{1,0:T(8,128)} %get-tuple-element.34.mask) | copy-start | bytes 196612
  75.0 10.4 %all-to-all-start.4 = ((f32[16,8,128]{2,1,0:T(8,128)}), f32[16,8,128]{2,1,0:T(8,128)S(1)}, u32[]{:S(2)}, u32[]{:S(2)}) async-start(f32[16,8,128]{2,1,0:T(8,128)} %get-tuple-element.35), calls=%async_computation.4 | async-start | bytes 131072 | tf_op jit(solution)/shard_map/all_to_all | solution.py:690
  78.5 55.0 %all-gather.5.cloned.1.call-start = ((), (), s32[]{:S(2)}) async-start(), calls=%async_computation.10 | async-start | bytes 2228224 | tf_op jit(solution)/shard_map/all_gather | solution.py:808
  89.8 11.6 %all-to-all-start.5 = ((bf16[16,32,128]{2,1,0:T(8,128)(2,1)}), bf16[16,32,128]{2,1,0:T(8,128)(2,1)S(1)}, u32[]{:S(2)}, u32[]{:S(2)}) async-start(bf16[16,32,128]{2,1,0:T(8,128)(2,1)} %get-tuple-element.40), calls=%async_computation.5 | async-start | bytes 262144 | tf_op jit(solution)/shard_map/all_to_all | solution.py:690
  101.4 15.1 %copy-start.1 = (bf16[16,8,128,128]{3,2,1,0:T(8,128)(2,1)S(1)}, bf16[16,8,128,128]{3,2,1,0:T(8,128)(2,1)}, u32[]{:S(2)}) copy-start(bf16[16,8,128,128]{3,2,1,0:T(8,128)(2,1)} %footprint.7) | copy-start | bytes 12582916
  130.0 10.4 %all-to-all-start.8 = ((f32[16,8,128]{2,1,0:T(8,128)}), f32[16,8,128]{2,1,0:T(8,128)S(1)}, u32[]{:S(2)}, u32[]{:S(2)}) async-start(f32[16,8,128]{2,1,0:T(8,128)} %get-tuple-element.45), calls=%async_computation.8 | async-start | bytes 131072 | tf_op jit(solution)/shard_map/all_to_all | solution.py:690
Sparse Core Ops, SparseCore 0:
  29.4 40.5 all-gather.2
  89.9 41.0 all-gather.4

commit v3 on v1

--- a/solution.py
+++ b/solution.py
@@ -205,16 +205,22 @@
 PIECES = 8
 
 
-def fetch(source, held, arrived):
+def fetch(source, held, arrived, ahead=None):
     pieces = arrived.shape[0]
     size = source.shape[0] // pieces
     copies = []
     for p in range(pieces):
         at = pl.ds(p * size, size)
         copies.append(pltpu.make_async_copy(source.at[at], held.at[at], arrived.at[p]))
-    for copy in copies:
+    for copy in copies[:ahead]:
         copy.start()
     return copies
+
+
+def arrive(copies, p, ahead):
+    copies[p].wait()
+    if p + ahead < len(copies):
+        copies[p + ahead].start()
 
 
 def second_of(tile_block):
@@ -268,7 +274,7 @@
     piece = owners // len(copies)
     for owner in range(owners):
         if owner % piece == 0:
-            copies[owner // piece].wait()
+            arrive(copies, owner // piece, 2)
         rows = vectors[owner, 0:8]
         lhs = rows.astype(jnp.bfloat16)
         if split:
@@ -297,9 +303,9 @@
     everyone, shelf, footprint,
     by_column, by_tile, products, held, arrived, mask_lon, shelf_arrived,
 ):
-    copies = fetch(footprint, held, arrived)
     shelf_copy = pltpu.make_async_copy(shelf.at[0:2], mask_lon, shelf_arrived)
     shelf_copy.start()
+    copies = fetch(footprint, held, arrived, 2)
     spread_tiles(everyone, held, copies, products, False)
     shelf_copy.wait()
     spread_end(products, mask_lon, by_column, by_tile)
@@ -328,9 +334,9 @@
     products, held, arrived, mask_lon, shelf_arrived,
 ):
     del after
-    copies = fetch(footprint, held, arrived)
     shelf_copy = pltpu.make_async_copy(shelf.at[0:2], mask_lon, shelf_arrived)
     shelf_copy.start()
+    copies = fetch(footprint, held, arrived, 2)
     first = everyone[:, 0:8, :]
     image = with_variance(image_in[...], everyone, first)
     norm_now = row_gram(first, first)
@@ -406,13 +412,13 @@
 
 def mix_body(columns, tile_prior, *rest):
     mixed, total, held, arrived = rest[-4:]
-    copies = fetch(tile_prior, held, arrived)
+    copies = fetch(tile_prior, held, arrived, 3)
     devices, width, tiles = columns.shape
     part = devices // len(copies)
-    for p, copy in enumerate(copies):
+    for p in range(len(copies)):
         at = range(p * part, (p + 1) * part)
         lhs = jnp.concatenate([columns[d] for d in at], axis=1)
-        copy.wait()
+        arrive(copies, p, 3)
         product = jnp.dot(
             lhs,
             held[p * part * tiles : (p + 1) * part * tiles],
@@ -615,7 +621,7 @@
     field = pltpu.VMEM(field_shape.shape, f32)
     gathered_held = pltpu.VMEM((every_tile, columns), bf16)
     prior_held = pltpu.VMEM(prior_shape.shape, bf16)
-    spread_scratch = [products, pltpu.VMEM(footprint.shape, bf16), flags(2 * PIECES)]
+    spread_scratch = [products, pltpu.VMEM(footprint.shape, bf16), flags(PIECES)]
     spread_scratch += [pltpu.VMEM((2, 128, 128), f32), pltpu.SemaphoreType.DMA]
     flux_scratch = [field, pltpu.VMEM(parts_shape.shape, f32), gathered_held]
     flux_scratch += [flags(1), flags(PIECES), flags(steps_here // 2)]

time: 153 us -> 157 us (1.026)
  Pallas kernels: 54.6 us -> 59.1 us
    pallas_call x2, Pallas kernels: 7.85 us -> 10.5 us  [prior(): call(mix_body, [vmem, hbm] + [hbm] * len(after), vmem, column_shape, [plt...]
  transfers between devices with their start and end apart: 6 -> 6, of which waited for: 3 -> 3; matrix products, arithmetic and copies ran while one was open for 0% -> 0% of each run, Pallas kernels for 24% -> 25%
where the time goes in v3:
time: 157 us; the launch traced here: 156 us
  blocking collectives  62 us (39%)
  Pallas kernels  59.1 us (38%)
  starting transfers between devices  14.3 us (9%)
  between operations  14.2 us (9%)
  waiting for transfers between devices  6.48 us (4%)
    all_to_all x5, blocking collectives, exchange(): return lax.all_to_all(array, 'tm', split_axis=0, concat_axis=0, tiled=True)  62 us
    all_to_all x4, starting transfers between devices, exchange(): return lax.all_to_all(array, 'tm', split_axis=0, concat_axis=0, tiled=True)  14.2 us
    pallas_call x2, Pallas kernels, prior(): call(mix_body, [vmem, hbm] + [hbm] * len(after), vmem, column_shape, [plt...  10.5 us
    pallas_call x2, Pallas kernels, flux_product(): call(functools.partial(flux_product_body, rows), [hbm, hbm, hbm], [hbm, v...  10.2 us
    pallas_call x1, Pallas kernels, by_columns(): call(build_body, [smem] + [vmem] * 3, [hbm, hbm], [prior_shape, parts_sha...  8.04 us
    pallas_call x1, Pallas kernels, by_columns(): call(update_body, [vmem] * 2 + [hbm] * 3, [vmem] * 5, [column_shape, tile...  6.46 us
    all_to_all x4, waiting for transfers between devices, exchange(): return lax.all_to_all(array, 'tm', split_axis=0, concat_axis=0, tiled=True)  6.41 us
    pallas_call x1, Pallas kernels, by_columns(): call(first_body, [vmem, hbm, hbm], [vmem] * 2, [column_shape, tile_shape]...  6.3 us
  transfers between devices with their start and end apart: 6, of which 3 were waited for; matrix products, arithmetic and copies ran while one was open for 0% of the time, Pallas kernels for 25%

profile of v3, /device:TPU:0, one launch (start us, length us, event | category | flops | bytes accessed | tf_op | source)
XLA Modules:
  0.0 156.1 jit_solution(10457917309742366849)
XLA Ops:
  7.2 0.0 all-gather.3.cloned.1.call-start
  7.2 2.5 %pack.1 = (f32[16,16,128]{2,1,0:T(8,128)}, f32[128,128]{1,0:T(8,128)}, f32[64,128,128]{2,1,0:T(8,128)}) custom-call(f32[2,4,128]{2,1,0:T(4,128)} %right_sides.1, f32[2,128]{1,0:T(2,128)} %obs_var.1, s32[8,16]{1,0:T(8,128)} %bitcast.3, s32[8,16]{1,0:T(8,128)} %bitcast.4, f32[128,128]{1,0:T(8,128)} %lon.1), custom_call_target="tpu_custom_call" | custom-call | bytes 12582912 | tf_op jit(solution)/shard_map/pack/pallas_call | solution.py:647
  9.7 15.3 %all_to_all.45.everyone = f32[16,16,128]{2,1,0:T(8,128)S(1)} all-to-all(f32[16,16,128]{2,1,0:T(8,128)} %get-tuple-element.23), channel_id=1, replica_groups=mesh['grp'=2,'tm'=16] {'tm'}, dimensions={0} | all-to-all | bytes 262144 | tf_op jit(solution)/shard_map/all_to_all | solution.py:644
  25.0 0.0 copy-start.3
  25.0 0.0 copy-start.4
  25.0 6.3 %spread_first.1 = (bf16[16,32,128]{2,1,0:T(8,128)(2,1)}, bf16[128,512]{1,0:T(8,128)(2,1)}) custom-call(f32[16,16,128]{2,1,0:T(8,128)S(1)} %all_to_all.45.everyone, f32[64,128,128]{2,1,0:T(8,128)} %get-tuple-element.24.shelf, bf16[16,8,128,128]{3,2,1,0:T(8,128)(2,1)} %footprint.7), custom_call_target="tpu_custom_call" | custom-call | flops 33554432 | bytes 4194304 | tf_op jit(solution)/shard_map/spread_first/pallas_call | solution.py:662
  31.3 0.0 all-gather.3.cloned.1.call-update
  31.3 3.5 %all-to-all-start.1 = ((bf16[16,32,128]{2,1,0:T(8,128)(2,1)}), bf16[16,32,128]{2,1,0:T(8,128)(2,1)S(1)}, u32[]{:S(2)}, u32[]{:S(2)}) async-start(bf16[16,32,128]{2,1,0:T(8,128)(2,1)} %get-tuple-element.25), calls=%async_computation.1 | async-start | bytes 262144 | tf_op jit(solution)/shard_map/all_to_all | solution.py:644
  34.9 0.0 copy-done.3
  34.9 0.0 copy-done.4
  34.9 8.0 %build_prior.1 = (bf16[2048,2048]{1,0:T(8,128)(2,1)}, f32[136,2048]{1,0:T(8,128)}) custom-call(s32[1]{0:T(128)} %bitcast.me, f32[16,16,128]{2,1,0:T(8,128)S(1)} %all_to_all.45.everyone, f32[128,128]{1,0:T(8,128)S(1)} %copy-done.3, f32[128,128]{1,0:T(8,128)S(1)} %copy-done.4), custom_call_target="tpu_custom_call" | custom-call | flops 4294967296 | bytes 8388608 | tf_op jit(solution)/shard_map/build_prior/pallas_call | solution.py:673
  42.9 0.0 all-to-all-done.1.columns
  42.9 0.0 copy-start
  43.0 0.0 copy-start.2
  43.0 5.5 %mix_columns.2 = bf16[16,32,128]{2,1,0:T(8,128)(2,1)S(1)} custom-call(bf16[16,32,128]{2,1,0:T(8,128)(2,1)S(1)} %all-to-all-done.1.columns, bf16[2048,2048]{1,0:T(8,128)(2,1)} %get-tuple-element.26.tile_prior), custom_call_target="tpu_custom_call" | custom-call | flops 268435456 | bytes 8388608 | tf_op jit(solution)/shard_map/mix_columns/pallas_call | solution.py:703
  48.5 15.8 %all_to_all.46.values = bf16[16,32,128]{2,1,0:T(8,128)(2,1)S(1)} all-to-all(bf16[16,32,128]{2,1,0:T(8,128)(2,1)S(1)} %mix_columns.2), channel_id=1, replica_groups=mesh['grp'=2,'tm'=16] {'tm'}, dimensions={0} | all-to-all | bytes 262144 | tf_op jit(solution)/shard_map/all_to_all | solution.py:644
  64.3 0.0 copy-done
  64.3 0.0 copy-done.2
  64.3 2.4 %collect.2 = f32[16,8,128]{2,1,0:T(8,128)S(1)} custom-call(bf16[16,32,128]{2,1,0:T(8,128)(2,1)S(1)} %all_to_all.46.values, f32[128,128]{1,0:T(8,128)S(1)} %copy-done.2, bf16[16,8,128,128]{3,2,1,0:T(8,128)(2,1)S(1)} %copy-done), custom_call_target="tpu_custom_call" | custom-call | flops 33554432 | bytes 4194304 | tf_op jit(solution)/shard_map/collect/pallas_call | solution.py:715
  66.7 9.9 %all_to_all.47.terms = f32[16,8,128]{2,1,0:T(8,128)S(1)} all-to-all(f32[16,8,128]{2,1,0:T(8,128)S(1)} %collect.2), channel_id=1, replica_groups=mesh['grp'=2,'tm'=16] {'tm'}, dimensions={0} | all-to-all | bytes 131072 | tf_op jit(solution)/shard_map/all_to_all | solution.py:644
  76.5 0.7 sum_terms.2
  77.2 3.5 %all-to-all-start.4 = ((f32[16,8,128]{2,1,0:T(8,128)}), f32[16,8,128]{2,1,0:T(8,128)S(1)}, u32[]{:S(2)}, u32[]{:S(2)}) async-start(f32[16,8,128]{2,1,0:T(8,128)} %get-tuple-element.28), calls=%async_computation.4 | async-start | bytes 131072 | tf_op jit(solution)/shard_map/all_to_all | solution.py:644
  80.7 0.0 all-gather.5.cloned.1.call-start
  80.7 0.0 all-gather.3.cloned.1.call-done.gathered
  80.8 4.2 %flux_product.2 = (f32[1024,512]{1,0:T(8,128)}, f32[8,128]{1,0:T(8,128)S(1)}) custom-call(f32[8,128]{1,0:T(8,128)S(1)} %get-tuple-element.29.after, f32[136,2048]{1,0:T(8,128)} %get-tuple-element.30.parts, bf16[2048,512]{1,0:T(8,128)(2,1)} %all-gather.3.cloned.1.call-done.gathered), custom_call_target="tpu_custom_call" | custom-call | flops 2147483648 | bytes 2097152 | tf_op jit(solution)/shard_map/flux_product/pallas_call | solution.py:692
  85.0 2.5 %all-to-all-done.4.image_in = f32[16,8,128]{2,1,0:T(8,128)S(1)} async-done(((f32[16,8,128]{2,1,0:T(8,128)}), f32[16,8,128]{2,1,0:T(8,128)S(1)}, u32[]{:S(2)}, u32[]{:S(2)}) %all-to-all-start.4) | async-done | bytes 65568 | tf_op jit(solution)/shard_map/all_to_all | solution.py:644
  87.5 6.5 %update_spread.1 = (bf16[16,32,128]{2,1,0:T(8,128)(2,1)}, bf16[128,512]{1,0:T(8,128)(2,1)}, f32[16,8,128]{2,1,0:T(8,128)S(1)}, f32[16,128]{1,0:T(8,128)S(1)}, f32[16,128]{1,0:T(8,128)S(1)}) custom-call(f32[16,16,128]{2,1,0:T(8,128)S(1)} %all_to_all.45.everyone, f32[16,8,128]{2,1,0:T(8,128)S(1)} %all-to-all-done.4.image_in, ...), custom_call_target="tpu_custom_call" | custom-call | flops 33554432 | bytes 4194304 | tf_op jit(solution)/shard_map/update_spread/pallas_call | solution.py:731
  94.0 0.0 all-gather.5.cloned.1.call-update
  94.0 3.7 %all-to-all-start.5 = ((bf16[16,32,128]{2,1,0:T(8,128)(2,1)}), bf16[16,32,128]{2,1,0:T(8,128)(2,1)S(1)}, u32[]{:S(2)}, u32[]{:S(2)}) async-start(bf16[16,32,128]{2,1,0:T(8,128)(2,1)} %get-tuple-element.33), calls=%async_computation.5 | async-start | bytes 262144 | tf_op jit(solution)/shard_map/all_to_all | solution.py:644
  97.7 4.7 %flux_first.1 = (f32[1024,512]{1,0:T(8,128)}, f32[8,128]{1,0:T(8,128)S(1)}) custom-call(f32[16,128]{1,0:T(8,128)S(1)} %get-tuple-element.34.sizes, f32[1024,512]{1,0:T(8,128)} %get-tuple-element.35.product, f32[136,2048]{1,0:T(8,128)} %get-tuple-element.30.parts, bf16[2048,512]{1,0:T(8,128)(2,1)} %all-gather.3.cloned.1.call-done.gathered), custom_call_target="tpu_custom_call" | custom-call | flops 2147483648 | bytes 2097152 | tf_op jit(solution)/shard_map/flux_first/pallas_call | solution.py:741
  102.5 3.0 %all-to-all-done.5.columns = bf16[16,32,128]{2,1,0:T(8,128)(2,1)S(1)} async-done(((bf16[16,32,128]{2,1,0:T(8,128)(2,1)}), bf16[16,32,128]{2,1,0:T(8,128)(2,1)S(1)}, u32[]{:S(2)}, u32[]{:S(2)}) %all-to-all-start.5) | async-done | bytes 131104 | tf_op jit(solution)/shard_map/all_to_all | solution.py:644
  105.5 0.0 copy-start.1
  105.5 5.0 %mix_columns.3 = bf16[16,32,128]{2,1,0:T(8,128)(2,1)S(1)} custom-call(bf16[16,32,128]{2,1,0:T(8,128)(2,1)S(1)} %all-to-all-done.5.columns, bf16[2048,2048]{1,0:T(8,128)(2,1)} %get-tuple-element.26.tile_prior, f32[8,128]{1,0:T(8,128)S(1)} %get-tuple-element.36.rest_0_), custom_call_target="tpu_custom_call" | custom-call | flops 268435456 | bytes 8388608 | tf_op jit(solution)/shard_map/mix_columns/pallas_call | solution.py:703
  110.4 10.7 %all_to_all.48.values = bf16[16,32,128]{2,1,0:T(8,128)(2,1)S(1)} all-to-all(bf16[16,32,128]{2,1,0:T(8,128)(2,1)S(1)} %mix_columns.3), channel_id=1, replica_groups=mesh['grp'=2,'tm'=16] {'tm'}, dimensions={0} | all-to-all | bytes 262144 | tf_op jit(solution)/shard_map/all_to_all | solution.py:644
  121.1 0.0 copy-done.1
  121.1 2.4 %collect.3 = f32[16,8,128]{2,1,0:T(8,128)S(1)} custom-call(bf16[16,32,128]{2,1,0:T(8,128)(2,1)S(1)} %all_to_all.48.values, f32[128,128]{1,0:T(8,128)S(1)} %copy-done.2, bf16[16,8,128,128]{3,2,1,0:T(8,128)(2,1)S(1)} %copy-done.1), custom_call_target="tpu_custom_call" | custom-call | flops 33554432 | bytes 4194304 | tf_op jit(solution)/shard_map/collect/pallas_call | solution.py:715
  123.5 10.3 %all_to_all.49.terms = f32[16,8,128]{2,1,0:T(8,128)S(1)} all-to-all(f32[16,8,128]{2,1,0:T(8,128)S(1)} %collect.3), channel_id=1, replica_groups=mesh['grp'=2,'tm'=16] {'tm'}, dimensions={0} | all-to-all | bytes 131072 | tf_op jit(solution)/shard_map/all_to_all | solution.py:644
  133.8 0.7 sum_terms.3
  134.4 3.5 %all-to-all-start.8 = ((f32[16,8,128]{2,1,0:T(8,128)}), f32[16,8,128]{2,1,0:T(8,128)S(1)}, u32[]{:S(2)}, u32[]{:S(2)}) async-start(f32[16,8,128]{2,1,0:T(8,128)} %get-tuple-element.37), calls=%async_computation.8 | async-start | bytes 131072 | tf_op jit(solution)/shard_map/all_to_all | solution.py:644
  137.9 0.0 all-gather.5.cloned.1.call-done.gathered
  138.0 5.9 %flux_product.3 = (f32[1024,512]{1,0:T(8,128)}, f32[8,128]{1,0:T(8,128)}) custom-call(f32[8,128]{1,0:T(8,128)S(1)} %get-tuple-element.41.after, f32[136,2048]{1,0:T(8,128)} %get-tuple-element.30.parts, bf16[2048,512]{1,0:T(8,128)(2,1)} %all-gather.5.cloned.1.call-done.gathered), custom_call_target="tpu_custom_call" | custom-call | flops 2147483648 | bytes 2097152 | tf_op jit(solution)/shard_map/flux_product/pallas_call | solution.py:692
  143.9 0.9 all-to-all-done.8.image_in
  144.8 4.4 %last.1 = (f32[2,4,128]{2,1,0:T(4,128)}, f32[8,128,4,128]{3,2,1,0:T(4,128)}) custom-call(s32[1]{0:T(128)} %bitcast.me, f32[16,16,128]{2,1,0:T(8,128)S(1)} %all_to_all.45.everyone, f32[16,8,128]{2,1,0:T(8,128)S(1)} %all-to-all-done.8.image_in, f32[16,8,128]{2,1,0:T(8,128)S(1)} %get-tuple-element.38.direction, f32[16,128]{1,0:T(8,128)S(1)} %get-tuple-element.34.sizes, ...), custom_call_target="tpu_custom_call" | custom-call | flops 1048576 | bytes 6291456 | tf_op jit(solution)/shard_map/last/pallas_call | solution.py:754
Async XLA Ops:
  7.2 73.6 %all-gather.3.cloned.1.call-start = ((), (), s32[]{:S(2)}) async-start(), calls=%async_computation.9 | async-start | bytes 2228224 | tf_op jit(solution)/shard_map/all_gather | solution.py:671
  25.0 9.9 %copy-start.3 = (f32[128,128]{1,0:T(8,128)S(1)}, f32[128,128]{1,0:T(8,128)}, u32[]{:S(2)}) copy-start(f32[128,128]{1,0:T(8,128)} %time_cov.1) | copy-start | bytes 196612
  25.0 9.9 %copy-start.4 = (f32[128,128]{1,0:T(8,128)S(1)}, f32[128,128]{1,0:T(8,128)}, u32[]{:S(2)}) copy-start(f32[128,128]{1,0:T(8,128)} %lat_cov.1) | copy-start | bytes 196612
  31.3 11.6 %all-to-all-start.1 = ((bf16[16,32,128]{2,1,0:T(8,128)(2,1)}), bf16[16,32,128]{2,1,0:T(8,128)(2,1)S(1)}, u32[]{:S(2)}, u32[]{:S(2)}) async-start(bf16[16,32,128]{2,1,0:T(8,128)(2,1)} %get-tuple-element.25), calls=%async_computation.1 | async-start | bytes 262144 | tf_op jit(solution)/shard_map/all_to_all | solution.py:644
  42.9 21.4 %copy-start = (bf16[16,8,128,128]{3,2,1,0:T(8,128)(2,1)S(1)}, bf16[16,8,128,128]{3,2,1,0:T(8,128)(2,1)}, u32[]{:S(2)}) copy-start(bf16[16,8,128,128]{3,2,1,0:T(8,128)(2,1)} %footprint.7) | copy-start | bytes 12582916
  43.0 21.4 %copy-start.2 = (f32[128,128]{1,0:T(8,128)S(1)}, f32[128,128]{1,0:T(8,128)}, u32[]{:S(2)}) copy-start(f32[128,128]{1,0:T(8,128)} %get-tuple-element.27.mask) | copy-start | bytes 196612
  77.2 10.4 %all-to-all-start.4 = ((f32[16,8,128]{2,1,0:T(8,128)}), f32[16,8,128]{2,1,0:T(8,128)S(1)}, u32[]{:S(2)}, u32[]{:S(2)}) async-start(f32[16,8,128]{2,1,0:T(8,128)} %get-tuple-element.28), calls=%async_computation.4 | async-start | bytes 131072 | tf_op jit(solution)/shard_map/all_to_all | solution.py:644
  80.7 57.3 %all-gather.5.cloned.1.call-start = ((), (), s32[]{:S(2)}) async-start(), calls=%async_computation.10 | async-start | bytes 2228224 | tf_op jit(solution)/shard_map/all_gather | solution.py:740
  94.0 11.4 %all-to-all-start.5 = ((bf16[16,32,128]{2,1,0:T(8,128)(2,1)}), bf16[16,32,128]{2,1,0:T(8,128)(2,1)S(1)}, u32[]{:S(2)}, u32[]{:S(2)}) async-start(bf16[16,32,128]{2,1,0:T(8,128)(2,1)} %get-tuple-element.33), calls=%async_computation.5 | async-start | bytes 262144 | tf_op jit(solution)/shard_map/all_to_all | solution.py:644
  105.5 15.7 %copy-start.1 = (bf16[16,8,128,128]{3,2,1,0:T(8,128)(2,1)S(1)}, bf16[16,8,128,128]{3,2,1,0:T(8,128)(2,1)}, u32[]{:S(2)}) copy-start(bf16[16,8,128,128]{3,2,1,0:T(8,128)(2,1)} %footprint.7) | copy-start | bytes 12582916
  134.4 10.4 %all-to-all-start.8 = ((f32[16,8,128]{2,1,0:T(8,128)}), f32[16,8,128]{2,1,0:T(8,128)S(1)}, u32[]{:S(2)}, u32[]{:S(2)}) async-start(f32[16,8,128]{2,1,0:T(8,128)} %get-tuple-element.37), calls=%async_computation.8 | async-start | bytes 131072 | tf_op jit(solution)/shard_map/all_to_all | solution.py:644
Sparse Core Ops, SparseCore 0:
  31.5 40.9 all-gather.2
  94.2 40.8 all-gather.4

commit v4 on v1

--- a/solution.py
+++ b/solution.py
@@ -297,9 +297,9 @@
     everyone, shelf, footprint,
     by_column, by_tile, products, held, arrived, mask_lon, shelf_arrived,
 ):
-    copies = fetch(footprint, held, arrived)
     shelf_copy = pltpu.make_async_copy(shelf.at[0:2], mask_lon, shelf_arrived)
     shelf_copy.start()
+    copies = fetch(footprint, held, arrived)
     spread_tiles(everyone, held, copies, products, False)
     shelf_copy.wait()
     spread_end(products, mask_lon, by_column, by_tile)
@@ -328,9 +328,9 @@
     products, held, arrived, mask_lon, shelf_arrived,
 ):
     del after
-    copies = fetch(footprint, held, arrived)
     shelf_copy = pltpu.make_async_copy(shelf.at[0:2], mask_lon, shelf_arrived)
     shelf_copy.start()
+    copies = fetch(footprint, held, arrived)
     first = everyone[:, 0:8, :]
     image = with_variance(image_in[...], everyone, first)
     norm_now = row_gram(first, first)
@@ -615,7 +615,7 @@
     field = pltpu.VMEM(field_shape.shape, f32)
     gathered_held = pltpu.VMEM((every_tile, columns), bf16)
     prior_held = pltpu.VMEM(prior_shape.shape, bf16)
-    spread_scratch = [products, pltpu.VMEM(footprint.shape, bf16), flags(2 * PIECES)]
+    spread_scratch = [products, pltpu.VMEM(footprint.shape, bf16), flags(4)]
     spread_scratch += [pltpu.VMEM((2, 128, 128), f32), pltpu.SemaphoreType.DMA]
     flux_scratch = [field, pltpu.VMEM(parts_shape.shape, f32), gathered_held]
     flux_scratch += [flags(1), flags(PIECES), flags(steps_here // 2)]

time: 153 us -> 150 us (0.980)
  Pallas kernels: 54.6 us -> 52.4 us
  transfers between devices with their start and end apart: 6 -> 6, of which waited for: 3 -> 3; matrix products, arithmetic and copies ran while one was open for 0% -> 0% of each run, Pallas kernels for 24% -> 25%
where the time goes in v4:
time: 150 us
  blocking collectives  62.2 us (41%)
  Pallas kernels  52.4 us (35%)
  starting transfers between devices  14.3 us (10%)
  between operations  14.2 us (9%)
  waiting for transfers between devices  6.48 us (4%)
    all_to_all x5, blocking collectives, exchange(): return lax.all_to_all(array, 'tm', split_axis=0, concat_axis=0, tiled=True)  62.2 us
    all_to_all x4, starting transfers between devices, exchange(): return lax.all_to_all(array, 'tm', split_axis=0, concat_axis=0, tiled=True)  14.2 us
    pallas_call x2, Pallas kernels, flux_product(): call(functools.partial(flux_product_body, rows), [hbm, hbm, hbm], [hbm, v...  10.2 us
    pallas_call x1, Pallas kernels, by_columns(): call(build_body, [smem] + [vmem] * 3, [hbm, hbm], [prior_shape, parts_sha...  8.03 us
    pallas_call x2, Pallas kernels, prior(): call(mix_body, [vmem, hbm] + [hbm] * len(after), vmem, column_shape, [plt...  7.85 us
    all_to_all x4, waiting for transfers between devices, exchange(): return lax.all_to_all(array, 'tm', split_axis=0, concat_axis=0, tiled=True)  6.41 us
    pallas_call x1, Pallas kernels, by_columns(): call(flux_first_body, [vmem, hbm, hbm, hbm], [hbm, vmem], [field_shape, t...  4.75 us
    pallas_call x2, Pallas kernels, collect(): call(collect_body, [vmem] * 3, vmem, vector_shape, [products], tile_cost,...  4.72 us
  transfers between devices with their start and end apart: 6, of which 3 were waited for; matrix products, arithmetic and copies ran while one was open for 0% of the time, Pallas kernels for 25%

profile of v4, /device:TPU:0, one launch (start us, length us, event | category | flops | bytes accessed | tf_op | source)
XLA Modules:
  0.0 149.6 jit_solution(15554566271446564257)
XLA Ops:
  7.2 0.0 all-gather.3.cloned.1.call-start
  7.2 2.5 %pack.1 = (f32[16,16,128]{2,1,0:T(8,128)}, f32[128,128]{1,0:T(8,128)}, f32[64,128,128]{2,1,0:T(8,128)}) custom-call(f32[2,4,128]{2,1,0:T(4,128)} %right_sides.1, f32[2,128]{1,0:T(2,128)} %obs_var.1, s32[8,16]{1,0:T(8,128)} %bitcast.3, s32[8,16]{1,0:T(8,128)} %bitcast.4, f32[128,128]{1,0:T(8,128)} %lon.1), custom_call_target="tpu_custom_call" | custom-call | bytes 12582912 | tf_op jit(solution)/shard_map/pack/pallas_call | solution.py:641
  9.7 15.3 %all_to_all.45.everyone = f32[16,16,128]{2,1,0:T(8,128)S(1)} all-to-all(f32[16,16,128]{2,1,0:T(8,128)} %get-tuple-element.23), channel_id=1, replica_groups=mesh['grp'=2,'tm'=16] {'tm'}, dimensions={0} | all-to-all | bytes 262144 | tf_op jit(solution)/shard_map/all_to_all | solution.py:638
  25.0 0.0 copy-start.3
  25.0 0.0 copy-start.4
  25.0 4.2 %spread_first.1 = (bf16[16,32,128]{2,1,0:T(8,128)(2,1)}, bf16[128,512]{1,0:T(8,128)(2,1)}) custom-call(f32[16,16,128]{2,1,0:T(8,128)S(1)} %all_to_all.45.everyone, f32[64,128,128]{2,1,0:T(8,128)} %get-tuple-element.24.shelf, bf16[16,8,128,128]{3,2,1,0:T(8,128)(2,1)} %footprint.7), custom_call_target="tpu_custom_call" | custom-call | flops 33554432 | bytes 4194304 | tf_op jit(solution)/shard_map/spread_first/pallas_call | solution.py:656
  29.3 0.0 all-gather.3.cloned.1.call-update
  29.3 3.5 %all-to-all-start.1 = ((bf16[16,32,128]{2,1,0:T(8,128)(2,1)}), bf16[16,32,128]{2,1,0:T(8,128)(2,1)S(1)}, u32[]{:S(2)}, u32[]{:S(2)}) async-start(bf16[16,32,128]{2,1,0:T(8,128)(2,1)} %get-tuple-element.25), calls=%async_computation.1 | async-start | bytes 262144 | tf_op jit(solution)/shard_map/all_to_all | solution.py:638
  32.8 0.0 copy-done.3
  32.8 0.0 copy-done.4
  32.8 8.0 %build_prior.1 = (bf16[2048,2048]{1,0:T(8,128)(2,1)}, f32[136,2048]{1,0:T(8,128)}) custom-call(s32[1]{0:T(128)} %bitcast.me, f32[16,16,128]{2,1,0:T(8,128)S(1)} %all_to_all.45.everyone, f32[128,128]{1,0:T(8,128)S(1)} %copy-done.3, f32[128,128]{1,0:T(8,128)S(1)} %copy-done.4), custom_call_target="tpu_custom_call" | custom-call | flops 4294967296 | bytes 8388608 | tf_op jit(solution)/shard_map/build_prior/pallas_call | solution.py:667
  40.9 0.0 all-to-all-done.1.columns
  40.9 0.0 copy-start
  40.9 0.0 copy-start.2
  40.9 3.9 %mix_columns.2 = bf16[16,32,128]{2,1,0:T(8,128)(2,1)S(1)} custom-call(bf16[16,32,128]{2,1,0:T(8,128)(2,1)S(1)} %all-to-all-done.1.columns, bf16[2048,2048]{1,0:T(8,128)(2,1)} %get-tuple-element.26.tile_prior), custom_call_target="tpu_custom_call" | custom-call | flops 268435456 | bytes 8388608 | tf_op jit(solution)/shard_map/mix_columns/pallas_call | solution.py:697
  44.8 15.6 %all_to_all.46.values = bf16[16,32,128]{2,1,0:T(8,128)(2,1)S(1)} all-to-all(bf16[16,32,128]{2,1,0:T(8,128)(2,1)S(1)} %mix_columns.2), channel_id=1, replica_groups=mesh['grp'=2,'tm'=16] {'tm'}, dimensions={0} | all-to-all | bytes 262144 | tf_op jit(solution)/shard_map/all_to_all | solution.py:638
  60.4 0.0 copy-done
  60.4 0.0 copy-done.2
  60.4 2.4 %collect.2 = f32[16,8,128]{2,1,0:T(8,128)S(1)} custom-call(bf16[16,32,128]{2,1,0:T(8,128)(2,1)S(1)} %all_to_all.46.values, f32[128,128]{1,0:T(8,128)S(1)} %copy-done.2, bf16[16,8,128,128]{3,2,1,0:T(8,128)(2,1)S(1)} %copy-done), custom_call_target="tpu_custom_call" | custom-call | flops 33554432 | bytes 4194304 | tf_op jit(solution)/shard_map/collect/pallas_call | solution.py:709
  62.8 10.1 %all_to_all.47.terms = f32[16,8,128]{2,1,0:T(8,128)S(1)} all-to-all(f32[16,8,128]{2,1,0:T(8,128)S(1)} %collect.2), channel_id=1, replica_groups=mesh['grp'=2,'tm'=16] {'tm'}, dimensions={0} | all-to-all | bytes 131072 | tf_op jit(solution)/shard_map/all_to_all | solution.py:638
  72.9 0.7 sum_terms.2
  73.5 3.5 %all-to-all-start.4 = ((f32[16,8,128]{2,1,0:T(8,128)}), f32[16,8,128]{2,1,0:T(8,128)S(1)}, u32[]{:S(2)}, u32[]{:S(2)}) async-start(f32[16,8,128]{2,1,0:T(8,128)} %get-tuple-element.28), calls=%async_computation.4 | async-start | bytes 131072 | tf_op jit(solution)/shard_map/all_to_all | solution.py:638
  77.0 0.0 all-gather.5.cloned.1.call-start
  77.1 0.0 all-gather.3.cloned.1.call-done.gathered
  77.1 4.2 %flux_product.2 = (f32[1024,512]{1,0:T(8,128)}, f32[8,128]{1,0:T(8,128)S(1)}) custom-call(f32[8,128]{1,0:T(8,128)S(1)} %get-tuple-element.29.after, f32[136,2048]{1,0:T(8,128)} %get-tuple-element.30.parts, bf16[2048,512]{1,0:T(8,128)(2,1)} %all-gather.3.cloned.1.call-done.gathered), custom_call_target="tpu_custom_call" | custom-call | flops 2147483648 | bytes 2097152 | tf_op jit(solution)/shard_map/flux_product/pallas_call | solution.py:686
  81.4 2.5 %all-to-all-done.4.image_in = f32[16,8,128]{2,1,0:T(8,128)S(1)} async-done(((f32[16,8,128]{2,1,0:T(8,128)}), f32[16,8,128]{2,1,0:T(8,128)S(1)}, u32[]{:S(2)}, u32[]{:S(2)}) %all-to-all-start.4) | async-done | bytes 65568 | tf_op jit(solution)/shard_map/all_to_all | solution.py:638
  83.9 4.4 %update_spread.1 = (bf16[16,32,128]{2,1,0:T(8,128)(2,1)}, bf16[128,512]{1,0:T(8,128)(2,1)}, f32[16,8,128]{2,1,0:T(8,128)S(1)}, f32[16,128]{1,0:T(8,128)S(1)}, f32[16,128]{1,0:T(8,128)S(1)}) custom-call(f32[16,16,128]{2,1,0:T(8,128)S(1)} %all_to_all.45.everyone, f32[16,8,128]{2,1,0:T(8,128)S(1)} %all-to-all-done.4.image_in, ...), custom_call_target="tpu_custom_call" | custom-call | flops 33554432 | bytes 4194304 | tf_op jit(solution)/shard_map/update_spread/pallas_call | solution.py:725
  88.3 0.0 all-gather.5.cloned.1.call-update
  88.3 3.7 %all-to-all-start.5 = ((bf16[16,32,128]{2,1,0:T(8,128)(2,1)}), bf16[16,32,128]{2,1,0:T(8,128)(2,1)S(1)}, u32[]{:S(2)}, u32[]{:S(2)}) async-start(bf16[16,32,128]{2,1,0:T(8,128)(2,1)} %get-tuple-element.33), calls=%async_computation.5 | async-start | bytes 262144 | tf_op jit(solution)/shard_map/all_to_all | solution.py:638
  92.1 4.7 %flux_first.1 = (f32[1024,512]{1,0:T(8,128)}, f32[8,128]{1,0:T(8,128)S(1)}) custom-call(f32[16,128]{1,0:T(8,128)S(1)} %get-tuple-element.34.sizes, f32[1024,512]{1,0:T(8,128)} %get-tuple-element.35.product, f32[136,2048]{1,0:T(8,128)} %get-tuple-element.30.parts, bf16[2048,512]{1,0:T(8,128)(2,1)} %all-gather.3.cloned.1.call-done.gathered), custom_call_target="tpu_custom_call" | custom-call | flops 2147483648 | bytes 2097152 | tf_op jit(solution)/shard_map/flux_first/pallas_call | solution.py:735
  96.8 3.0 %all-to-all-done.5.columns = bf16[16,32,128]{2,1,0:T(8,128)(2,1)S(1)} async-done(((bf16[16,32,128]{2,1,0:T(8,128)(2,1)}), bf16[16,32,128]{2,1,0:T(8,128)(2,1)S(1)}, u32[]{:S(2)}, u32[]{:S(2)}) %all-to-all-start.5) | async-done | bytes 131104 | tf_op jit(solution)/shard_map/all_to_all | solution.py:638
  99.8 0.0 copy-start.1
  99.8 3.9 %mix_columns.3 = bf16[16,32,128]{2,1,0:T(8,128)(2,1)S(1)} custom-call(bf16[16,32,128]{2,1,0:T(8,128)(2,1)S(1)} %all-to-all-done.5.columns, bf16[2048,2048]{1,0:T(8,128)(2,1)} %get-tuple-element.26.tile_prior, f32[8,128]{1,0:T(8,128)S(1)} %get-tuple-element.36.rest_0_), custom_call_target="tpu_custom_call" | custom-call | flops 268435456 | bytes 8388608 | tf_op jit(solution)/shard_map/mix_columns/pallas_call | solution.py:697
  103.7 10.7 %all_to_all.48.values = bf16[16,32,128]{2,1,0:T(8,128)(2,1)S(1)} all-to-all(bf16[16,32,128]{2,1,0:T(8,128)(2,1)S(1)} %mix_columns.3), channel_id=1, replica_groups=mesh['grp'=2,'tm'=16] {'tm'}, dimensions={0} | all-to-all | bytes 262144 | tf_op jit(solution)/shard_map/all_to_all | solution.py:638
  114.4 0.0 copy-done.1
  114.4 2.4 %collect.3 = f32[16,8,128]{2,1,0:T(8,128)S(1)} custom-call(bf16[16,32,128]{2,1,0:T(8,128)(2,1)S(1)} %all_to_all.48.values, f32[128,128]{1,0:T(8,128)S(1)} %copy-done.2, bf16[16,8,128,128]{3,2,1,0:T(8,128)(2,1)S(1)} %copy-done.1), custom_call_target="tpu_custom_call" | custom-call | flops 33554432 | bytes 4194304 | tf_op jit(solution)/shard_map/collect/pallas_call | solution.py:709
  116.8 10.5 %all_to_all.49.terms = f32[16,8,128]{2,1,0:T(8,128)S(1)} all-to-all(f32[16,8,128]{2,1,0:T(8,128)S(1)} %collect.3), channel_id=1, replica_groups=mesh['grp'=2,'tm'=16] {'tm'}, dimensions={0} | all-to-all | bytes 131072 | tf_op jit(solution)/shard_map/all_to_all | solution.py:638
  127.3 0.7 sum_terms.3
  127.9 3.5 %all-to-all-start.8 = ((f32[16,8,128]{2,1,0:T(8,128)}), f32[16,8,128]{2,1,0:T(8,128)S(1)}, u32[]{:S(2)}, u32[]{:S(2)}) async-start(f32[16,8,128]{2,1,0:T(8,128)} %get-tuple-element.37), calls=%async_computation.8 | async-start | bytes 131072 | tf_op jit(solution)/shard_map/all_to_all | solution.py:638
  131.4 0.0 all-gather.5.cloned.1.call-done.gathered
  131.5 5.9 %flux_product.3 = (f32[1024,512]{1,0:T(8,128)}, f32[8,128]{1,0:T(8,128)}) custom-call(f32[8,128]{1,0:T(8,128)S(1)} %get-tuple-element.41.after, f32[136,2048]{1,0:T(8,128)} %get-tuple-element.30.parts, bf16[2048,512]{1,0:T(8,128)(2,1)} %all-gather.5.cloned.1.call-done.gathered), custom_call_target="tpu_custom_call" | custom-call | flops 2147483648 | bytes 2097152 | tf_op jit(solution)/shard_map/flux_product/pallas_call | solution.py:686
  137.4 0.9 all-to-all-done.8.image_in
  138.3 4.4 %last.1 = (f32[2,4,128]{2,1,0:T(4,128)}, f32[8,128,4,128]{3,2,1,0:T(4,128)}) custom-call(s32[1]{0:T(128)} %bitcast.me, f32[16,16,128]{2,1,0:T(8,128)S(1)} %all_to_all.45.everyone, f32[16,8,128]{2,1,0:T(8,128)S(1)} %all-to-all-done.8.image_in, f32[16,8,128]{2,1,0:T(8,128)S(1)} %get-tuple-element.38.direction, f32[16,128]{1,0:T(8,128)S(1)} %get-tuple-element.34.sizes, ...), custom_call_target="tpu_custom_call" | custom-call | flops 1048576 | bytes 6291456 | tf_op jit(solution)/shard_map/last/pallas_call | solution.py:748
Async XLA Ops:
  7.2 69.9 %all-gather.3.cloned.1.call-start = ((), (), s32[]{:S(2)}) async-start(), calls=%async_computation.9 | async-start | bytes 2228224 | tf_op jit(solution)/shard_map/all_gather | solution.py:665
  25.0 7.8 %copy-start.3 = (f32[128,128]{1,0:T(8,128)S(1)}, f32[128,128]{1,0:T(8,128)}, u32[]{:S(2)}) copy-start(f32[128,128]{1,0:T(8,128)} %time_cov.1) | copy-start | bytes 196612
  25.0 7.8 %copy-start.4 = (f32[128,128]{1,0:T(8,128)S(1)}, f32[128,128]{1,0:T(8,128)}, u32[]{:S(2)}) copy-start(f32[128,128]{1,0:T(8,128)} %lat_cov.1) | copy-start | bytes 196612
  29.3 11.6 %all-to-all-start.1 = ((bf16[16,32,128]{2,1,0:T(8,128)(2,1)}), bf16[16,32,128]{2,1,0:T(8,128)(2,1)S(1)}, u32[]{:S(2)}, u32[]{:S(2)}) async-start(bf16[16,32,128]{2,1,0:T(8,128)(2,1)} %get-tuple-element.25), calls=%async_computation.1 | async-start | bytes 262144 | tf_op jit(solution)/shard_map/all_to_all | solution.py:638
  40.9 19.5 %copy-start = (bf16[16,8,128,128]{3,2,1,0:T(8,128)(2,1)S(1)}, bf16[16,8,128,128]{3,2,1,0:T(8,128)(2,1)}, u32[]{:S(2)}) copy-start(bf16[16,8,128,128]{3,2,1,0:T(8,128)(2,1)} %footprint.7) | copy-start | bytes 12582916
  40.9 19.5 %copy-start.2 = (f32[128,128]{1,0:T(8,128)S(1)}, f32[128,128]{1,0:T(8,128)}, u32[]{:S(2)}) copy-start(f32[128,128]{1,0:T(8,128)} %get-tuple-element.27.mask) | copy-start | bytes 196612
  73.5 10.4 %all-to-all-start.4 = ((f32[16,8,128]{2,1,0:T(8,128)}), f32[16,8,128]{2,1,0:T(8,128)S(1)}, u32[]{:S(2)}, u32[]{:S(2)}) async-start(f32[16,8,128]{2,1,0:T(8,128)} %get-tuple-element.28), calls=%async_computation.4 | async-start | bytes 131072 | tf_op jit(solution)/shard_map/all_to_all | solution.py:638
  77.0 54.4 %all-gather.5.cloned.1.call-start = ((), (), s32[]{:S(2)}) async-start(), calls=%async_computation.10 | async-start | bytes 2228224 | tf_op jit(solution)/shard_map/all_gather | solution.py:734
  88.3 11.4 %all-to-all-start.5 = ((bf16[16,32,128]{2,1,0:T(8,128)(2,1)}), bf16[16,32,128]{2,1,0:T(8,128)(2,1)S(1)}, u32[]{:S(2)}, u32[]{:S(2)}) async-start(bf16[16,32,128]{2,1,0:T(8,128)(2,1)} %get-tuple-element.33), calls=%async_computation.5 | async-start | bytes 262144 | tf_op jit(solution)/shard_map/all_to_all | solution.py:638
  99.8 14.6 %copy-start.1 = (bf16[16,8,128,128]{3,2,1,0:T(8,128)(2,1)S(1)}, bf16[16,8,128,128]{3,2,1,0:T(8,128)(2,1)}, u32[]{:S(2)}) copy-start(bf16[16,8,128,128]{3,2,1,0:T(8,128)(2,1)} %footprint.7) | copy-start | bytes 12582916
  127.9 10.4 %all-to-all-start.8 = ((f32[16,8,128]{2,1,0:T(8,128)}), f32[16,8,128]{2,1,0:T(8,128)S(1)}, u32[]{:S(2)}, u32[]{:S(2)}) async-start(f32[16,8,128]{2,1,0:T(8,128)} %get-tuple-element.37), calls=%async_computation.8 | async-start | bytes 131072 | tf_op jit(solution)/shard_map/all_to_all | solution.py:638
Sparse Core Ops, SparseCore 0:
  29.4 39.9 all-gather.2
  88.5 40.6 all-gather.4

commit v5 on v4

--- a/solution.py
+++ b/solution.py
@@ -279,14 +279,24 @@
             products[owner * slots + c] = r[:8] + r[8:] if split else r
 
 
+def halves(x):
+    upper = x.astype(jnp.bfloat16)
+    return upper, (x - upper.astype(jnp.float32)).astype(jnp.bfloat16)
+
+
 def spread_end(products, mask_lon, by_column, by_tile):
     second = mask_lon[0] > 0.5
+    upper, lower = halves(mask_lon[1])
+    lon = jnp.concatenate([upper, upper, lower], axis=0)
     width = by_column.shape[1]
     chunks = LON // width
     for k in range(SAMPLES):
         chosen = jnp.where(second, products[:, 2 * k + 1, :], products[:, 2 * k, :])
+        upper, lower = halves(chosen)
         mixed = jnp.dot(
-            chosen, mask_lon[1], precision=precise, preferred_element_type=jnp.float32
+            jnp.concatenate([upper, lower, upper], axis=1),
+            lon,
+            preferred_element_type=jnp.float32,
         )
         by_tile[:, k * LON : (k + 1) * LON] = mixed.astype(jnp.bfloat16)
         turned = mixed.T.astype(jnp.bfloat16)

time: 150 us -> 150 us (level)
  no operation moved by 1% of the time
where the time goes in v5:
time: 150 us; the launch traced here: 149 us
  blocking collectives  62.2 us (41%)
  Pallas kernels  52 us (35%)
  starting transfers between devices  14.3 us (10%)
  between operations  14.2 us (9%)
  waiting for transfers between devices  6.48 us (4%)
    all_to_all x5, blocking collectives, exchange(): return lax.all_to_all(array, 'tm', split_axis=0, concat_axis=0, tiled=True)  62.2 us
    all_to_all x4, starting transfers between devices, exchange(): return lax.all_to_all(array, 'tm', split_axis=0, concat_axis=0, tiled=True)  14.2 us
    pallas_call x2, Pallas kernels, flux_product(): call(functools.partial(flux_product_body, rows), [hbm, hbm, hbm], [hbm, v...  10.2 us
    pallas_call x1, Pallas kernels, by_columns(): call(build_body, [smem] + [vmem] * 3, [hbm, hbm], [prior_shape, parts_sha...  8.04 us
    pallas_call x2, Pallas kernels, prior(): call(mix_body, [vmem, hbm] + [hbm] * len(after), vmem, column_shape, [plt...  7.85 us
    all_to_all x4, waiting for transfers between devices, exchange(): return lax.all_to_all(array, 'tm', split_axis=0, concat_axis=0, tiled=True)  6.4 us
    pallas_call x1, Pallas kernels, by_columns(): call(flux_first_body, [vmem, hbm, hbm, hbm], [hbm, vmem], [field_shape, t...  4.75 us
    pallas_call x2, Pallas kernels, collect(): call(collect_body, [vmem] * 3, vmem, vector_shape, [products], tile_cost,...  4.72 us
  transfers between devices with their start and end apart: 6, of which 3 were waited for; matrix products, arithmetic and copies ran while one was open for 0% of the time, Pallas kernels for 25%

profile of v5, /device:TPU:0, one launch (start us, length us, event | category | flops | bytes accessed | tf_op | source)
XLA Modules:
  0.0 149.2 jit_solution(660524753130732276)
XLA Ops:
  7.2 0.0 all-gather.3.cloned.1.call-start
  7.2 2.5 %pack.1 = (f32[16,16,128]{2,1,0:T(8,128)}, f32[128,128]{1,0:T(8,128)}, f32[64,128,128]{2,1,0:T(8,128)}) custom-call(f32[2,4,128]{2,1,0:T(4,128)} %right_sides.1, f32[2,128]{1,0:T(2,128)} %obs_var.1, s32[8,16]{1,0:T(8,128)} %bitcast.3, s32[8,16]{1,0:T(8,128)} %bitcast.4, f32[128,128]{1,0:T(8,128)} %lon.1), custom_call_target="tpu_custom_call" | custom-call | bytes 12582912 | tf_op jit(solution)/shard_map/pack/pallas_call | solution.py:651
  9.7 15.3 %all_to_all.45.everyone = f32[16,16,128]{2,1,0:T(8,128)S(1)} all-to-all(f32[16,16,128]{2,1,0:T(8,128)} %get-tuple-element.23), channel_id=1, replica_groups=mesh['grp'=2,'tm'=16] {'tm'}, dimensions={0} | all-to-all | bytes 262144 | tf_op jit(solution)/shard_map/all_to_all | solution.py:648
  25.0 0.0 copy-start.3
  25.0 0.0 copy-start.4
  25.0 4.1 %spread_first.1 = (bf16[16,32,128]{2,1,0:T(8,128)(2,1)}, bf16[128,512]{1,0:T(8,128)(2,1)}) custom-call(f32[16,16,128]{2,1,0:T(8,128)S(1)} %all_to_all.45.everyone, f32[64,128,128]{2,1,0:T(8,128)} %get-tuple-element.24.shelf, bf16[16,8,128,128]{3,2,1,0:T(8,128)(2,1)} %footprint.7), custom_call_target="tpu_custom_call" | custom-call | flops 33554432 | bytes 4194304 | tf_op jit(solution)/shard_map/spread_first/pallas_call | solution.py:666
  29.1 0.0 all-gather.3.cloned.1.call-update
  29.1 3.5 %all-to-all-start.1 = ((bf16[16,32,128]{2,1,0:T(8,128)(2,1)}), bf16[16,32,128]{2,1,0:T(8,128)(2,1)S(1)}, u32[]{:S(2)}, u32[]{:S(2)}) async-start(bf16[16,32,128]{2,1,0:T(8,128)(2,1)} %get-tuple-element.25), calls=%async_computation.1 | async-start | bytes 262144 | tf_op jit(solution)/shard_map/all_to_all | solution.py:648
  32.6 0.0 copy-done.3
  32.6 0.0 copy-done.4
  32.7 8.0 %build_prior.1 = (bf16[2048,2048]{1,0:T(8,128)(2,1)}, f32[136,2048]{1,0:T(8,128)}) custom-call(s32[1]{0:T(128)} %bitcast.me, f32[16,16,128]{2,1,0:T(8,128)S(1)} %all_to_all.45.everyone, f32[128,128]{1,0:T(8,128)S(1)} %copy-done.3, f32[128,128]{1,0:T(8,128)S(1)} %copy-done.4), custom_call_target="tpu_custom_call" | custom-call | flops 4294967296 | bytes 8388608 | tf_op jit(solution)/shard_map/build_prior/pallas_call | solution.py:677
  40.7 0.0 all-to-all-done.1.columns
  40.7 0.0 copy-start
  40.7 0.0 copy-start.2
  40.7 3.9 %mix_columns.2 = bf16[16,32,128]{2,1,0:T(8,128)(2,1)S(1)} custom-call(bf16[16,32,128]{2,1,0:T(8,128)(2,1)S(1)} %all-to-all-done.1.columns, bf16[2048,2048]{1,0:T(8,128)(2,1)} %get-tuple-element.26.tile_prior), custom_call_target="tpu_custom_call" | custom-call | flops 268435456 | bytes 8388608 | tf_op jit(solution)/shard_map/mix_columns/pallas_call | solution.py:707
  44.7 15.6 %all_to_all.46.values = bf16[16,32,128]{2,1,0:T(8,128)(2,1)S(1)} all-to-all(bf16[16,32,128]{2,1,0:T(8,128)(2,1)S(1)} %mix_columns.2), channel_id=1, replica_groups=mesh['grp'=2,'tm'=16] {'tm'}, dimensions={0} | all-to-all | bytes 262144 | tf_op jit(solution)/shard_map/all_to_all | solution.py:648
  60.3 0.0 copy-done
  60.3 0.0 copy-done.2
  60.3 2.4 %collect.2 = f32[16,8,128]{2,1,0:T(8,128)S(1)} custom-call(bf16[16,32,128]{2,1,0:T(8,128)(2,1)S(1)} %all_to_all.46.values, f32[128,128]{1,0:T(8,128)S(1)} %copy-done.2, bf16[16,8,128,128]{3,2,1,0:T(8,128)(2,1)S(1)} %copy-done), custom_call_target="tpu_custom_call" | custom-call | flops 33554432 | bytes 4194304 | tf_op jit(solution)/shard_map/collect/pallas_call | solution.py:719
  62.6 10.1 %all_to_all.47.terms = f32[16,8,128]{2,1,0:T(8,128)S(1)} all-to-all(f32[16,8,128]{2,1,0:T(8,128)S(1)} %collect.2), channel_id=1, replica_groups=mesh['grp'=2,'tm'=16] {'tm'}, dimensions={0} | all-to-all | bytes 131072 | tf_op jit(solution)/shard_map/all_to_all | solution.py:648
  72.7 0.7 sum_terms.2
  73.4 3.5 %all-to-all-start.4 = ((f32[16,8,128]{2,1,0:T(8,128)}), f32[16,8,128]{2,1,0:T(8,128)S(1)}, u32[]{:S(2)}, u32[]{:S(2)}) async-start(f32[16,8,128]{2,1,0:T(8,128)} %get-tuple-element.28), calls=%async_computation.4 | async-start | bytes 131072 | tf_op jit(solution)/shard_map/all_to_all | solution.py:648
  76.8 0.0 all-gather.5.cloned.1.call-start
  76.9 0.0 all-gather.3.cloned.1.call-done.gathered
  76.9 4.2 %flux_product.2 = (f32[1024,512]{1,0:T(8,128)}, f32[8,128]{1,0:T(8,128)S(1)}) custom-call(f32[8,128]{1,0:T(8,128)S(1)} %get-tuple-element.29.after, f32[136,2048]{1,0:T(8,128)} %get-tuple-element.30.parts, bf16[2048,512]{1,0:T(8,128)(2,1)} %all-gather.3.cloned.1.call-done.gathered), custom_call_target="tpu_custom_call" | custom-call | flops 2147483648 | bytes 2097152 | tf_op jit(solution)/shard_map/flux_product/pallas_call | solution.py:696
  81.2 2.5 %all-to-all-done.4.image_in = f32[16,8,128]{2,1,0:T(8,128)S(1)} async-done(((f32[16,8,128]{2,1,0:T(8,128)}), f32[16,8,128]{2,1,0:T(8,128)S(1)}, u32[]{:S(2)}, u32[]{:S(2)}) %all-to-all-start.4) | async-done | bytes 65568 | tf_op jit(solution)/shard_map/all_to_all | solution.py:648
  83.7 4.2 %update_spread.1 = (bf16[16,32,128]{2,1,0:T(8,128)(2,1)}, bf16[128,512]{1,0:T(8,128)(2,1)}, f32[16,8,128]{2,1,0:T(8,128)S(1)}, f32[16,128]{1,0:T(8,128)S(1)}, f32[16,128]{1,0:T(8,128)S(1)}) custom-call(f32[16,16,128]{2,1,0:T(8,128)S(1)} %all_to_all.45.everyone, f32[16,8,128]{2,1,0:T(8,128)S(1)} %all-to-all-done.4.image_in, ...), custom_call_target="tpu_custom_call" | custom-call | flops 33554432 | bytes 4194304 | tf_op jit(solution)/shard_map/update_spread/pallas_call | solution.py:735
  88.0 0.0 all-gather.5.cloned.1.call-update
  88.0 3.7 %all-to-all-start.5 = ((bf16[16,32,128]{2,1,0:T(8,128)(2,1)}), bf16[16,32,128]{2,1,0:T(8,128)(2,1)S(1)}, u32[]{:S(2)}, u32[]{:S(2)}) async-start(bf16[16,32,128]{2,1,0:T(8,128)(2,1)} %get-tuple-element.33), calls=%async_computation.5 | async-start | bytes 262144 | tf_op jit(solution)/shard_map/all_to_all | solution.py:648
  91.7 4.8 %flux_first.1 = (f32[1024,512]{1,0:T(8,128)}, f32[8,128]{1,0:T(8,128)S(1)}) custom-call(f32[16,128]{1,0:T(8,128)S(1)} %get-tuple-element.34.sizes, f32[1024,512]{1,0:T(8,128)} %get-tuple-element.35.product, f32[136,2048]{1,0:T(8,128)} %get-tuple-element.30.parts, bf16[2048,512]{1,0:T(8,128)(2,1)} %all-gather.3.cloned.1.call-done.gathered), custom_call_target="tpu_custom_call" | custom-call | flops 2147483648 | bytes 2097152 | tf_op jit(solution)/shard_map/flux_first/pallas_call | solution.py:745
  96.5 3.0 %all-to-all-done.5.columns = bf16[16,32,128]{2,1,0:T(8,128)(2,1)S(1)} async-done(((bf16[16,32,128]{2,1,0:T(8,128)(2,1)}), bf16[16,32,128]{2,1,0:T(8,128)(2,1)S(1)}, u32[]{:S(2)}, u32[]{:S(2)}) %all-to-all-start.5) | async-done | bytes 131104 | tf_op jit(solution)/shard_map/all_to_all | solution.py:648
  99.4 0.0 copy-start.1
  99.4 3.9 %mix_columns.3 = bf16[16,32,128]{2,1,0:T(8,128)(2,1)S(1)} custom-call(bf16[16,32,128]{2,1,0:T(8,128)(2,1)S(1)} %all-to-all-done.5.columns, bf16[2048,2048]{1,0:T(8,128)(2,1)} %get-tuple-element.26.tile_prior, f32[8,128]{1,0:T(8,128)S(1)} %get-tuple-element.36.rest_0_), custom_call_target="tpu_custom_call" | custom-call | flops 268435456 | bytes 8388608 | tf_op jit(solution)/shard_map/mix_columns/pallas_call | solution.py:707
  103.4 10.7 %all_to_all.48.values = bf16[16,32,128]{2,1,0:T(8,128)(2,1)S(1)} all-to-all(bf16[16,32,128]{2,1,0:T(8,128)(2,1)S(1)} %mix_columns.3), channel_id=1, replica_groups=mesh['grp'=2,'tm'=16] {'tm'}, dimensions={0} | all-to-all | bytes 262144 | tf_op jit(solution)/shard_map/all_to_all | solution.py:648
  114.1 0.0 copy-done.1
  114.1 2.4 %collect.3 = f32[16,8,128]{2,1,0:T(8,128)S(1)} custom-call(bf16[16,32,128]{2,1,0:T(8,128)(2,1)S(1)} %all_to_all.48.values, f32[128,128]{1,0:T(8,128)S(1)} %copy-done.2, bf16[16,8,128,128]{3,2,1,0:T(8,128)(2,1)S(1)} %copy-done.1), custom_call_target="tpu_custom_call" | custom-call | flops 33554432 | bytes 4194304 | tf_op jit(solution)/shard_map/collect/pallas_call | solution.py:719
  116.4 10.5 %all_to_all.49.terms = f32[16,8,128]{2,1,0:T(8,128)S(1)} all-to-all(f32[16,8,128]{2,1,0:T(8,128)S(1)} %collect.3), channel_id=1, replica_groups=mesh['grp'=2,'tm'=16] {'tm'}, dimensions={0} | all-to-all | bytes 131072 | tf_op jit(solution)/shard_map/all_to_all | solution.py:648
  126.9 0.7 sum_terms.3
  127.6 3.5 %all-to-all-start.8 = ((f32[16,8,128]{2,1,0:T(8,128)}), f32[16,8,128]{2,1,0:T(8,128)S(1)}, u32[]{:S(2)}, u32[]{:S(2)}) async-start(f32[16,8,128]{2,1,0:T(8,128)} %get-tuple-element.37), calls=%async_computation.8 | async-start | bytes 131072 | tf_op jit(solution)/shard_map/all_to_all | solution.py:648
  131.1 0.0 all-gather.5.cloned.1.call-done.gathered
  131.1 5.9 %flux_product.3 = (f32[1024,512]{1,0:T(8,128)}, f32[8,128]{1,0:T(8,128)}) custom-call(f32[8,128]{1,0:T(8,128)S(1)} %get-tuple-element.41.after, f32[136,2048]{1,0:T(8,128)} %get-tuple-element.30.parts, bf16[2048,512]{1,0:T(8,128)(2,1)} %all-gather.5.cloned.1.call-done.gathered), custom_call_target="tpu_custom_call" | custom-call | flops 2147483648 | bytes 2097152 | tf_op jit(solution)/shard_map/flux_product/pallas_call | solution.py:696
  137.0 0.9 all-to-all-done.8.image_in
  137.9 4.4 %last.1 = (f32[2,4,128]{2,1,0:T(4,128)}, f32[8,128,4,128]{3,2,1,0:T(4,128)}) custom-call(s32[1]{0:T(128)} %bitcast.me, f32[16,16,128]{2,1,0:T(8,128)S(1)} %all_to_all.45.everyone, f32[16,8,128]{2,1,0:T(8,128)S(1)} %all-to-all-done.8.image_in, f32[16,8,128]{2,1,0:T(8,128)S(1)} %get-tuple-element.38.direction, f32[16,128]{1,0:T(8,128)S(1)} %get-tuple-element.34.sizes, ...), custom_call_target="tpu_custom_call" | custom-call | flops 1048576 | bytes 6291456 | tf_op jit(solution)/shard_map/last/pallas_call | solution.py:758
Async XLA Ops:
  7.2 69.7 %all-gather.3.cloned.1.call-start = ((), (), s32[]{:S(2)}) async-start(), calls=%async_computation.9 | async-start | bytes 2228224 | tf_op jit(solution)/shard_map/all_gather | solution.py:675
  25.0 7.6 %copy-start.3 = (f32[128,128]{1,0:T(8,128)S(1)}, f32[128,128]{1,0:T(8,128)}, u32[]{:S(2)}) copy-start(f32[128,128]{1,0:T(8,128)} %time_cov.1) | copy-start | bytes 196612
  25.0 7.6 %copy-start.4 = (f32[128,128]{1,0:T(8,128)S(1)}, f32[128,128]{1,0:T(8,128)}, u32[]{:S(2)}) copy-start(f32[128,128]{1,0:T(8,128)} %lat_cov.1) | copy-start | bytes 196612
  29.1 11.6 %all-to-all-start.1 = ((bf16[16,32,128]{2,1,0:T(8,128)(2,1)}), bf16[16,32,128]{2,1,0:T(8,128)(2,1)S(1)}, u32[]{:S(2)}, u32[]{:S(2)}) async-start(bf16[16,32,128]{2,1,0:T(8,128)(2,1)} %get-tuple-element.25), calls=%async_computation.1 | async-start | bytes 262144 | tf_op jit(solution)/shard_map/all_to_all | solution.py:648
  40.7 19.6 %copy-start = (bf16[16,8,128,128]{3,2,1,0:T(8,128)(2,1)S(1)}, bf16[16,8,128,128]{3,2,1,0:T(8,128)(2,1)}, u32[]{:S(2)}) copy-start(bf16[16,8,128,128]{3,2,1,0:T(8,128)(2,1)} %footprint.7) | copy-start | bytes 12582916
  40.7 19.5 %copy-start.2 = (f32[128,128]{1,0:T(8,128)S(1)}, f32[128,128]{1,0:T(8,128)}, u32[]{:S(2)}) copy-start(f32[128,128]{1,0:T(8,128)} %get-tuple-element.27.mask) | copy-start | bytes 196612
  73.4 10.4 %all-to-all-start.4 = ((f32[16,8,128]{2,1,0:T(8,128)}), f32[16,8,128]{2,1,0:T(8,128)S(1)}, u32[]{:S(2)}, u32[]{:S(2)}) async-start(f32[16,8,128]{2,1,0:T(8,128)} %get-tuple-element.28), calls=%async_computation.4 | async-start | bytes 131072 | tf_op jit(solution)/shard_map/all_to_all | solution.py:648
  76.8 54.3 %all-gather.5.cloned.1.call-start = ((), (), s32[]{:S(2)}) async-start(), calls=%async_computation.10 | async-start | bytes 2228224 | tf_op jit(solution)/shard_map/all_gather | solution.py:744
  88.0 11.4 %all-to-all-start.5 = ((bf16[16,32,128]{2,1,0:T(8,128)(2,1)}), bf16[16,32,128]{2,1,0:T(8,128)(2,1)S(1)}, u32[]{:S(2)}, u32[]{:S(2)}) async-start(bf16[16,32,128]{2,1,0:T(8,128)(2,1)} %get-tuple-element.33), calls=%async_computation.5 | async-start | bytes 262144 | tf_op jit(solution)/shard_map/all_to_all | solution.py:648
  99.4 14.6 %copy-start.1 = (bf16[16,8,128,128]{3,2,1,0:T(8,128)(2,1)S(1)}, bf16[16,8,128,128]{3,2,1,0:T(8,128)(2,1)}, u32[]{:S(2)}) copy-start(bf16[16,8,128,128]{3,2,1,0:T(8,128)(2,1)} %footprint.7) | copy-start | bytes 12582916
  127.6 10.4 %all-to-all-start.8 = ((f32[16,8,128]{2,1,0:T(8,128)}), f32[16,8,128]{2,1,0:T(8,128)S(1)}, u32[]{:S(2)}, u32[]{:S(2)}) async-start(f32[16,8,128]{2,1,0:T(8,128)} %get-tuple-element.37), calls=%async_computation.8 | async-start | bytes 131072 | tf_op jit(solution)/shard_map/all_to_all | solution.py:648
Sparse Core Ops, SparseCore 0:
  29.2 39.9 all-gather.2
  88.1 40.6 all-gather.4
